TPU v7x, 32 devices: a whole 2x2x4 slice. The times are simulated.
32 devices in a mesh: fsdp: 16 (over z, x, core), tok: 2 (over y).
Axes of the slice: x: 2, y: 2, z: 4, core: 2. Of those that a mesh axis runs over, the one named last changes fastest.
Arguments:
- tokens: bfloat16 [2048, 2048], P('fsdp', 'tok'), may hold values from -6 to 6
- expert_ids: int32 [2048, 4], P('fsdp'), may hold values from 0 to 31, all different within a row; in each aligned block of 128 rows (0 to 127, 128 to 255, ...) at most 32 rows name the same one
- gate_probs: float32 [2048, 4], P('fsdp'), may hold values from 0.05 to 1
- w_gate: bfloat16 [32, 1408, 2048], P('fsdp', 'tok'), may hold values from -0.125 to 0.125
- w_up: bfloat16 [32, 1408, 2048], P('fsdp', 'tok'), may hold values from -0.125 to 0.125
- w_down: bfloat16 [32, 1408, 2048], P('fsdp', 'tok'), may hold values from -0.15625 to 0.15625
- grad_out: bfloat16 [2048, 2048], P('fsdp', 'tok'), may hold values from -6 to 6
Outputs:
- layer_out: bfloat16 [2048, 2048], P('fsdp', 'tok')
- d_tokens: bfloat16 [2048, 2048], P('fsdp', 'tok')
- d_gate_probs: float32 [2048, 4], P('fsdp')
- d_w_gate: float32 [32, 1408, 2048], P('fsdp', 'tok')
- d_w_up: float32 [32, 1408, 2048], P('fsdp', 'tok')
- d_w_down: float32 [32, 1408, 2048], P('fsdp', 'tok')
Inputs may be any that keep to these rules, and one draw needn't show every extreme that they name: `expert_ids`: each token names 4 different experts. Among the tokens of one index of fsdp (aligned blocks of 128 tokens) no expert is named more than 32 times, a bound that some block reaches.
All inputs are finite; a program needn't handle non-finite values.
Results may differ from a plain program's by a relative error of at most 0.0064.
Values may be sent and summed in bfloat16 or wider, within the bound.
A program may use at most 128 MiB of HBM per device.

v0:
```python
import functools

import jax
import jax.numpy as jnp
from jax import lax
from jax.experimental import pallas as pl
from jax.experimental.pallas import tpu as pltpu
from jax.sharding import PartitionSpec as P

CAP = 32
MESH = pl.DeviceIdType.MESH


def flip(bit, change):
    return 1 - bit if change else bit


class Place:
    def __init__(self):
        f = lax.axis_index("fsdp")
        self.t = lax.axis_index("tok")
        self.core = f % 2
        self.x = (f // 2) % 2
        self.z0 = (f // 4) % 2
        self.z1 = f // 8

    def block(self, dz=0, dx=0, dc=0):
        z = flip(self.z1, dz // 2) * 2 + flip(self.z0, dz % 2)
        return z * 4 + flip(self.x, dx) * 2 + flip(self.core, dc)

    def device(self, dz=0, dx=0, dy=0, dc=0):
        return (self.block(dz, dx, dc), flip(self.t, dy))

    def columns(self, dy, width):
        return pl.ds(pl.multiple_of(flip(self.t, dy) * width, width), width)

    def partners(self):
        return [self.device(dz=d) for d in (1, 2, 3)] + [
            self.device(dx=1),
            self.device(dy=1),
            self.device(dc=1),
        ]


def greet(place):
    barrier = pltpu.get_barrier_semaphore()
    partners = place.partners()
    for partner in partners:
        pl.semaphore_signal(barrier, inc=1, device_id=partner, device_id_type=MESH)
    pl.semaphore_wait(barrier, len(partners))


def gather_kernel(in0, in1, out0, out1, send_sem, recv_sem, core_sem, own_sem):
    place = Place()
    ins, outs = (in0, in1), (out0, out1)
    rows, width = in0.shape
    half = rows // 2
    sent = []

    def where(a, h, dz, dx, dy, dc=0):
        return outs[a].at[
            place.block(dz, dx, dc), pl.ds(h * half, half), place.columns(dy, width)
        ]

    def send(a, h, dz, dx, dy, to, sem):
        own = dz == dx == dy == 0
        source = ins[a].at[pl.ds(h * half, half)] if own else where(a, h, dz, dx, dy)
        copy = pltpu.make_async_remote_copy(
            src_ref=source,
            dst_ref=where(a, h, dz, dx, dy),
            send_sem=send_sem.at[len(sent)],
            recv_sem=sem,
            device_id=to,
            device_id_type=MESH,
        )
        copy.start()
        sent.append(copy)

    def index(a, h, dz, dx, dy):
        return (((a * 2 + h) * 4 + dz) * 2 + dx) * 2 + dy

    def wait(a, h, dz, dx, dy, dc=0):
        place_here = where(a, h, dz, dx, dy, dc)
        sem = (core_sem if dc else recv_sem).at[index(a, h, dz, dx, dy)]
        pltpu.make_async_copy(place_here, place_here, sem).wait()

    def to_core(a, h, dz, dx, dy):
        send(a, h, dz, dx, dy, place.device(dc=1), core_sem.at[index(a, h, dz, dx, dy)])

    def to_x(a, h, dz, dy):
        send(a, h, dz, 0, dy, place.device(dx=1), recv_sem.at[index(a, h, dz, 1, dy)])

    def to_y(a, h, dz, dx):
        send(a, h, dz, dx, 0, place.device(dy=1), recv_sem.at[index(a, h, dz, dx, 1)])

    own_copies = [
        pltpu.make_async_copy(
            ins[a], outs[a].at[place.block(), :, place.columns(0, width)], own_sem.at[a]
        )
        for a in range(2)
    ]
    for copy in own_copies:
        copy.start()
    greet(place)
    events = []
    for a in range(2):
        for h in range(2):
            for dz in range(1, 4):
                events.append((a * 3, "z", a, h, dz))
            for dz in range(4):
                events.append((a * 30 + dz * 5 + 1, "column", a, h, dz))
                events.append((a * 30 + dz * 5 + 12, "plane", a, h, dz))
                events.append((a * 30 + dz * 5 + 22, "last", a, h, dz))
    for _, kind, a, h, dz in sorted(events):
        if kind == "z":
            send(a, h, 0, 0, 0, place.device(dz=dz), recv_sem.at[index(a, h, dz, 0, 0)])
        elif kind == "column":
            if dz:
                wait(a, h, dz, 0, 0)
            if h == 0:
                to_x(a, h, dz, 0)
                to_y(a, h, dz, 0)
            else:
                to_y(a, h, dz, 0)
                to_x(a, h, dz, 0)
            to_core(a, h, dz, 0, 0)
        elif kind == "plane":
            if h == 0:
                wait(a, h, dz, 1, 0)
                to_y(a, h, dz, 1)
                to_core(a, h, dz, 1, 0)
            else:
                wait(a, h, dz, 0, 1)
                to_x(a, h, dz, 1)
                to_core(a, h, dz, 0, 1)
        else:
            dx, dy = (0, 1) if h == 0 else (1, 0)
            wait(a, h, dz, dx, dy)
            to_core(a, h, dz, dx, dy)
            wait(a, h, dz, 1, 1)
            to_core(a, h, dz, 1, 1)
    for a in range(2):
        for h in range(2):
            for dz in range(4):
                for dx in range(2):
                    for dy in range(2):
                        wait(a, h, dz, dx, dy, 1)
    for copy in sent:
        copy.wait_send()
    for copy in own_copies:
        copy.wait()


def gather_pair(first, second):
    rows, width = first.shape
    full = jax.ShapeDtypeStruct((16, rows, 2 * width), first.dtype)
    return pl.pallas_call(
        gather_kernel,
        out_shape=(full, full),
        in_specs=[pl.BlockSpec(memory_space=pl.ANY)] * 2,
        out_specs=[pl.BlockSpec(memory_space=pl.ANY)] * 2,
        scratch_shapes=[
            pltpu.SemaphoreType.DMA((124,)),
            pltpu.SemaphoreType.DMA((64,)),
            pltpu.SemaphoreType.DMA((64,)),
            pltpu.SemaphoreType.DMA((2,)),
        ],
        compiler_params=pltpu.CompilerParams(collective_id=0, has_side_effects=True),
    )(first, second)


def scatter_kernel(
    in0, in1, out0, out1, core_buf, wide_buf, near_buf, z_buf, send_sem, core_sem, wide_sem, near_sem, z_sem
):
    place = Place()
    ins, outs = (in0, in1), (out0, out1)
    half, width = core_buf.shape[-2:]
    sent = []

    def send(source, target, sem, to):
        copy = pltpu.make_async_remote_copy(
            src_ref=source,
            dst_ref=target,
            send_sem=send_sem.at[len(sent)],
            recv_sem=sem,
            device_id=to,
            device_id_type=MESH,
        )
        copy.start()
        sent.append(copy)

    def arrive(buffer, sem):
        pltpu.make_async_copy(buffer, buffer, sem).wait()

    def add(target, source):
        def step(i, carry):
            at = pl.ds(pl.multiple_of(i * 16, 16), 16)
            target[at, :] = target[at, :] + source[at, :]
            return carry

        lax.fori_loop(0, half // 16, step, 0)

    def part(a, h, dz, dx, dy, dc):
        return ins[a].at[
            place.block(dz, dx, dc), pl.ds(h * half, half), place.columns(dy, width)
        ]

    def slot(a, h, dz, dx, dy):
        return (((a * 2 + h) * 4 + dz) * 2 + dx) * 2 + dy

    greet(place)
    order = [3, 2, 1, 0]
    events = []
    for a in range(2):
        for n, dz in enumerate(order):
            for h in range(2):
                events.append((a * 30 + n * 2 - 40, "core", a, h, dz))
                events.append((a * 30 + n * 6 + 4, "wide", a, h, dz))
                events.append((a * 30 + n * 6 + 14, "near", a, h, dz))
                events.append((a * 30 + n * 6 + 22, "z", a, h, dz))
    for _, kind, a, h, dz in sorted(events):
        pair = (a * 2 + h) * 4 + dz
        across = place.device(dy=1) if h == 0 else place.device(dx=1)
        along = place.device(dx=1) if h == 0 else place.device(dy=1)
        if kind == "core":
            for far in (1, 0):
                for other in (1, 0):
                    dx, dy = (other, far) if h == 0 else (far, other)
                    k = slot(a, h, dz, dx, dy)
                    send(part(a, h, dz, dx, dy, 1), core_buf.at[k], core_sem.at[k], place.device(dc=1))
        elif kind == "wide":
            for far in (1, 0):
                for other in (1, 0):
                    dx, dy = (other, far) if h == 0 else (far, other)
                    k = slot(a, h, dz, dx, dy)
                    arrive(core_buf.at[k], core_sem.at[k])
                    add(core_buf.at[k], part(a, h, dz, dx, dy, 0))
                    if far:
                        w = pair * 2 + other
                        send(core_buf.at[k], wide_buf.at[w], wide_sem.at[w], across)
        elif kind == "near":
            for other in (1, 0):
                dx, dy = (other, 0) if h == 0 else (0, other)
                w = pair * 2 + other
                arrive(wide_buf.at[w], wide_sem.at[w])
                add(wide_buf.at[w], core_buf.at[slot(a, h, dz, dx, dy)])
                if other:
                    send(wide_buf.at[w], near_buf.at[pair], near_sem.at[pair], along)
        else:
            arrive(near_buf.at[pair], near_sem.at[pair])
            add(near_buf.at[pair], wide_buf.at[pair * 2])
            if dz:
                send(near_buf.at[pair], z_buf.at[pair], z_sem.at[pair], place.device(dz=dz))
    for a in range(2):
        for h in range(2):
            pair = (a * 2 + h) * 4
            for dz in (3, 2, 1):
                arrive(z_buf.at[pair + dz], z_sem.at[pair + dz])

            def step(i, carry, a=a, h=h, pair=pair):
                at = pl.ds(pl.multiple_of(i * 16, 16), 16)
                total = near_buf[pair, at, :].astype(jnp.float32)
                for dz in (1, 2, 3):
                    total = total + z_buf[pair + dz, at, :].astype(jnp.float32)
                to = pl.ds(pl.multiple_of(h * half + i * 16, 16), 16)
                outs[a][to, :] = total.astype(outs[a].dtype)
                return carry

            lax.fori_loop(0, half // 16, step, 0)
    for copy in sent:
        copy.wait_send()


def scatter_pair(first, second):
    blocks, rows, full = first.shape
    half, width = rows // 2, full // 2
    out = jax.ShapeDtypeStruct((rows, width), first.dtype)
    return pl.pallas_call(
        scatter_kernel,
        out_shape=(out, out),
        in_specs=[pl.BlockSpec(memory_space=pltpu.VMEM)] * 2,
        out_specs=[pl.BlockSpec(memory_space=pltpu.VMEM)] * 2,
        scratch_shapes=[
            pltpu.VMEM((64, half, width), first.dtype),
            pltpu.VMEM((32, half, width), first.dtype),
            pltpu.VMEM((16, half, width), first.dtype),
            pltpu.VMEM((16, half, width), first.dtype),
            pltpu.SemaphoreType.DMA((124,)),
            pltpu.SemaphoreType.DMA((64,)),
            pltpu.SemaphoreType.DMA((32,)),
            pltpu.SemaphoreType.DMA((16,)),
            pltpu.SemaphoreType.DMA((16,)),
        ],
        compiler_params=pltpu.CompilerParams(
            collective_id=1, has_side_effects=True, vmem_limit_bytes=48 * 2**20
        ),
    )(first, second)


def gather_any(value):
    wide = lax.all_gather(value, "tok", axis=1, tiled=True)
    return lax.all_gather(wide, "fsdp", axis=0, tiled=False)


def scatter_any(value):
    blocks, rows, full = value.shape
    mine = lax.psum_scatter(
        value.reshape(blocks * rows, full), "fsdp", scatter_dimension=0, tiled=True
    )
    return lax.psum_scatter(mine, "tok", scatter_dimension=1, tiled=True)


def on_device(by_kernel, tokens, expert_ids, gate_probs, w_gate, w_up, w_down, grad_out):
    tok_rows, topk = expert_ids.shape
    local = w_gate.shape[0]
    f32 = jnp.float32
    me = lax.axis_index("fsdp")

    routes = jnp.concatenate([expert_ids.astype(f32).T, gate_probs.T], axis=0)
    routes = lax.all_gather(routes, "fsdp", axis=0, tiled=False)
    if by_kernel:
        all_tokens, all_grads = gather_pair(tokens, grad_out)
    else:
        all_tokens, all_grads = gather_any(tokens), gather_any(grad_out)
    blocks = all_tokens.shape[0]

    names = routes[:, :topk]
    mine = (me * local + jnp.arange(local, dtype=jnp.int32)).astype(f32)
    chosen = names[None] == mine[:, None, None, None]
    hit = jnp.any(chosen, axis=2)
    prob = jnp.sum(jnp.where(chosen, routes[None, :, topk:], 0.0), axis=2)
    before = jnp.triu(jnp.ones((tok_rows, tok_rows), jnp.bfloat16), 1)
    place = jnp.einsum("ebs,st->ebt", hit.astype(jnp.bfloat16), before, preferred_element_type=f32)
    place = jnp.where(hit, place, -1.0)
    filled = place[:, :, None, :] == jnp.arange(CAP, dtype=jnp.int32).astype(f32)[None, None, :, None]
    select = filled.astype(jnp.bfloat16)
    row_prob = jnp.sum(jnp.where(filled, prob[:, :, None, :], 0.0), axis=3)
    row_prob = row_prob.reshape(local, blocks * CAP, 1)

    def pick(values):
        rows = jnp.einsum("ebrt,btd->ebrd", select, values, preferred_element_type=f32)
        return rows.astype(jnp.bfloat16).reshape(local, blocks * CAP, values.shape[-1])

    def place_back(rows):
        rows = rows.astype(jnp.bfloat16).reshape(local, blocks, CAP, rows.shape[-1])
        values = jnp.einsum("ebrt,ebrd->btd", select, rows, preferred_element_type=f32)
        return values.astype(jnp.bfloat16)

    inputs = pick(all_tokens)
    cotangent = pick(all_grads)
    gate = jnp.einsum("erd,ehd->erh", inputs, w_gate, preferred_element_type=f32)
    upper = jnp.einsum("erd,ehd->erh", inputs, w_up, preferred_element_type=f32)
    raw = jnp.einsum("erd,ehd->erh", cotangent, w_down, preferred_element_type=f32)
    sigma = jax.nn.sigmoid(gate)
    active = gate * sigma
    hidden = active * upper
    weighted = (row_prob * hidden).astype(jnp.bfloat16)
    d_hidden = row_prob * raw
    d_gate = (d_hidden * upper * sigma * (1.0 + gate * (1.0 - sigma))).astype(jnp.bfloat16)
    d_upper = (d_hidden * active).astype(jnp.bfloat16)
    d_rows = jnp.sum(hidden * raw, axis=2).reshape(local, blocks, CAP)

    out_rows = jnp.einsum("erh,ehd->erd", weighted, w_down, preferred_element_type=f32)
    in_rows = jnp.einsum("erh,ehd->erd", d_gate, w_gate, preferred_element_type=f32)
    in_rows = in_rows + jnp.einsum("erh,ehd->erd", d_upper, w_up, preferred_element_type=f32)
    part_out, part_in = place_back(out_rows), place_back(in_rows)
    if by_kernel:
        layer_out, d_tokens = scatter_pair(part_out, part_in)
    else:
        layer_out, d_tokens = scatter_any(part_out), scatter_any(part_in)

    d_w_down = jnp.einsum("erh,erd->ehd", weighted, cotangent, preferred_element_type=f32)
    d_w_gate = jnp.einsum("erh,erd->ehd", d_gate, inputs, preferred_element_type=f32)
    d_w_up = jnp.einsum("erh,erd->ehd", d_upper, inputs, preferred_element_type=f32)

    d_prob = jnp.sum(jnp.where(filled, d_rows[:, :, :, None], 0.0), axis=2)
    d_prob = jnp.sum(jnp.where(chosen, d_prob[:, :, None, :], 0.0), axis=0)
    d_prob = d_prob.reshape(blocks, topk * tok_rows)
    d_prob = lax.all_to_all(d_prob, "fsdp", split_axis=0, concat_axis=0, tiled=True)
    d_prob = jnp.sum(d_prob, axis=0)
    size = lax.axis_size("tok")
    mine_only = d_prob
    for turn in range(1, size):
        pairs = [(i, (i + turn) % size) for i in range(size)]
        d_prob = d_prob + lax.ppermute(mine_only, "tok", pairs)
    d_gate_probs = d_prob.reshape(topk, tok_rows).T
    return (layer_out, d_tokens, d_gate_probs, d_w_gate, d_w_up, d_w_down)


def solution(mesh):
    by_kernel = mesh.shape["fsdp"] == 16 and mesh.shape["tok"] == 2
    return jax.shard_map(
        functools.partial(on_device, by_kernel),
        mesh=mesh,
        in_specs=(
            P("fsdp", "tok"),
            P("fsdp", None),
            P("fsdp", None),
            P("fsdp", "tok", None),
            P("fsdp", "tok", None),
            P("fsdp", "tok", None),
            P("fsdp", "tok"),
        ),
        out_specs=(
            P("fsdp", "tok"),
            P("fsdp", "tok"),
            P("fsdp", None),
            P("fsdp", "tok", None),
            P("fsdp", "tok", None),
            P("fsdp", "tok", None),
        ),
        check_vma=False,
    )
```

profile of v0, /device:TPU:0, one launch (start us, length us, event | category | flops | bytes accessed | tf_op | source)
XLA Modules:
  0.0 296.4 jit_solution(18321603893037328756)
XLA Ops:
  0.7 0.7 convert_bitcast_fusion.2
  1.3 0.7 pad_maximum_fusion
  2.0 23.2 %all-gather = f32[128,128]{1,0:T(8,128)S(1)} all-gather(f32[8,128]{1,0:T(8,128)S(1)} %pad_maximum_fusion), channel_id=2, replica_groups=mesh['fsdp'=16,'tok'=2] {'fsdp'}, dimensions={0}, use_global_device_ids=true | all-gather | bytes 69632 | tf_op jit(solution)/shard_map/all_gather | solution.py:320
  25.3 0.1 compare_reduce_fusion
  25.4 0.1 convolution_select_fusion
  25.5 83.7 %shard_map.118 = (bf16[16,128,2048]{2,1,0:T(8,128)(2,1)}, bf16[16,128,2048]{2,1,0:T(8,128)(2,1)}) custom-call(bf16[128,1024]{1,0:T(8,128)(2,1)} %in0.1, bf16[128,1024]{1,0:T(8,128)(2,1)} %in1.1), custom_call_target="tpu_custom_call" | custom-call | tf_op jit(solution)/shard_map/pallas_call | solution.py:157
  109.2 4.7 %convert_bitcast_fusion.1 = bf16[2,16,32,2048]{3,2,0,1:T(8,128)(2,1)S(1)} fusion(bf16[16,128,2048]{2,1,0:T(8,128)(2,1)} %get-tuple-element.10, f32[2,16,128]{2,0,1:T(2,128)S(1)} %copy.49, f32[32]{0:T(128)S(1)} %iota_convert_fusion), kind=kOutput, calls=%fused_computation.10 | convolution fusion | flops 539099136 | bytes 12599424 | tf_op jit(solution)/shard_map/ebrt,btd->ebrd/dot_general | solution.py:341
  113.9 0.0 slice-start
  113.9 0.3 copy.53
  114.3 0.0 copy-start
  114.3 0.0 slice-start.1
  114.3 7.2 %fusion.36 = f32[2,512,704]{1,2,0:T(8,128)S(1)} fusion(bf16[2,512,2048]{2,1,0:T(8,128)(2,1)S(1)} %bitcast.61, bf16[2,704,2048]{2,1,0:T(8,128)(2,1)} %param.11), kind=kOutput, calls=%fused_computation.54 | convolution fusion | flops 2952790016 | bytes 12845056 | tf_op jit(solution)/shard_map/erd,ehd->erh/dot_general | solution.py:352
  121.5 0.0 copy-done
  121.5 0.0 slice-done
  121.5 0.0 slice-done.1
  121.5 4.7 %fusion.35 = f32[2,512,704]{1,2,0:T(8,128)} fusion(bf16[2,512,2048]{2,1,0:T(8,128)(2,1)S(1)} %bitcast.62, bf16[2,704,2048]{2,1,0:T(8,128)(2,1)S(1)} %bitcast.70), kind=kOutput, calls=%fused_computation.53 | convolution fusion | flops 2952790016 | bytes 12845056 | tf_op jit(solution)/shard_map/erd,ehd->erh/dot_general | solution.py:351
  126.3 4.7 %convert_bitcast_fusion = bf16[2,16,32,2048]{3,2,0,1:T(8,128)(2,1)S(1)} fusion(bf16[16,128,2048]{2,1,0:T(8,128)(2,1)} %get-tuple-element.11, f32[2,16,128]{2,0,1:T(2,128)S(1)} %copy.49, f32[32]{0:T(128)S(1)} %iota_convert_fusion), kind=kOutput, calls=%fused_computation.9 | convolution fusion | flops 539099136 | bytes 12599424 | tf_op jit(solution)/shard_map/ebrt,btd->ebrd/dot_general | solution.py:341
  130.9 0.0 copy-start.4
  131.0 0.3 copy.55
  131.3 0.0 copy-start.2
  131.3 2.8 copy-done.4
  134.1 8.0 %multiply_reduce_fusion = (f32[2,512]{1,0:T(2,128)S(1)}, f32[2,512,704]{1,2,0:T(8,128)}) fusion(f32[2,512,704]{1,2,0:T(8,128)S(1)} %fusion.36, f32[2,512,704]{1,2,0:T(8,128)S(1)} %copy-done.4, bf16[2,512,2048]{2,1,0:T(8,128)(2,1)S(1)} %bitcast.65, bf16[2,704,2048]{2,1,0:T(8,128)(2,1)} %param.12), kind=kOutput, calls=%fused_computation.12 | convolution fusion | flops 2957835264 | bytes 18616320 | tf_op jit(solution)/shard_map/erd,ehd->erh/dot_general | solution.py:353
  142.1 0.0 copy-done.2
  142.1 0.1 broadcast_in_dim.71
  142.2 0.2 fusion.16
  142.4 0.1 fusion.26
  142.5 0.6 copy.59
  143.2 5.1 %all-to-all-start = ((f32[16,1,512]{2,1,0:T(1,128)}), f32[16,1,512]{2,1,0:T(1,128)S(1)}, u32[]{:S(2)}, u32[]{:S(2)}) async-start(f32[16,1,512]{2,1,0:T(1,128)} %bitcast.18), calls=%async_computation | async-start | bytes 65536 | tf_op jit(solution)/shard_map/all_to_all | solution.py:379
  148.3 0.3 fusion.15
  148.6 0.1 mul.44
  148.7 0.0 slice-start.2
  148.7 3.7 %multiply_convert_fusion = (bf16[2,512,704]{1,2,0:T(8,128)(2,1)S(1)}, bf16[2,512,704]{1,2,0:T(8,128)(2,1)S(1)}, bf16[2,512,704]{1,2,0:T(8,128)(2,1)S(1)}) fusion(f32[2,512,704]{1,2,0:T(8,128)} %get-tuple-element.22, f32[2,512]{1,0:T(2,128)S(1)} %mul.44, f32[2,512,704]{1,2,0:T(8,128)} %fusion.35, f32[2,512,704]{1,2,0:T(8,128)S(1)} %fusion.36), kind=kLoop, calls=%fused_computation.13 | loop fusion | flops 12255232 | bytes 12980224 | tf_op jit(solution)/shard_map/convert_element_type | solution.py:360
  152.5 0.0 copy-start.3
  152.5 0.0 slice-start.3
  152.5 6.5 %convolution_convert_fusion = bf16[2,512,2048]{2,1,0:T(8,128)(2,1)S(1)} fusion(bf16[2,512,704]{1,2,0:T(8,128)(2,1)S(1)} %get-tuple-element.18, bf16[2,704,2048]{2,1,0:T(8,128)(2,1)} %param.12), kind=kOutput, calls=%fused_computation.11 | convolution fusion | flops 2954887168 | bytes 11403264 | tf_op jit(solution)/shard_map/erh,ehd->erd/dot_general | solution.py:363
  159.0 0.0 copy-done.3
  159.0 6.1 %fusion.40 = f32[2,704,2048]{2,1,0:T(8,128)} fusion(bf16[2,512,704]{1,2,0:T(8,128)(2,1)S(1)} %get-tuple-element.18, bf16[2,512,2048]{2,1,0:T(8,128)(2,1)S(1)} %bitcast.66), kind=kOutput, calls=%fused_computation.58 | convolution fusion | flops 2952790016 | bytes 17170432 | tf_op jit(solution)/shard_map/erh,erd->ehd/dot_general | solution.py:372
  165.2 0.0 slice-done.2
  165.2 0.0 slice-done.3
  165.2 0.0 copy-start.1
  165.2 3.6 %fusion.37 = f32[2,512,2048]{2,1,0:T(8,128)S(1)} fusion(bf16[2,512,704]{1,2,0:T(8,128)(2,1)S(1)} %get-tuple-element.17, bf16[2,704,2048]{2,1,0:T(8,128)(2,1)S(1)} %bitcast.72), kind=kOutput, calls=%fused_computation.55 | convolution fusion | flops 2952790016 | bytes 15597568 | tf_op jit(solution)/shard_map/erh,ehd->erd/dot_general | solution.py:364
  168.8 0.0 copy-done.1
  168.8 0.0 slice-start.4
  168.8 6.1 %fusion.38 = f32[2,704,2048]{2,1,0:T(8,128)} fusion(bf16[2,512,704]{1,2,0:T(8,128)(2,1)S(1)} %get-tuple-element.17, bf16[2,512,2048]{2,1,0:T(8,128)(2,1)S(1)} %bitcast.63), kind=kOutput, calls=%fused_computation.56 | convolution fusion | flops 2952790016 | bytes 17170432 | tf_op jit(solution)/shard_map/erh,erd->ehd/dot_general | solution.py:373
  174.9 0.0 slice-start.5
  174.9 6.1 %fusion.39 = f32[2,704,2048]{2,1,0:T(8,128)} fusion(bf16[2,512,704]{1,2,0:T(8,128)(2,1)S(1)} %get-tuple-element.16, bf16[2,512,2048]{2,1,0:T(8,128)(2,1)S(1)} %bitcast.64), kind=kOutput, calls=%fused_computation.57 | convolution fusion | flops 2952790016 | bytes 17170432 | tf_op jit(solution)/shard_map/erh,erd->ehd/dot_general | solution.py:374
  181.0 0.0 slice-done.4
  181.0 0.0 slice-done.5
  181.0 5.3 %add_convert_fusion = bf16[2,512,2048]{2,1,0:T(8,128)(2,1)} fusion(f32[2,512,2048]{2,1,0:T(8,128)S(1)} %fusion.37, bf16[2,512,704]{1,2,0:T(8,128)(2,1)S(1)} %get-tuple-element.16, bf16[2,704,2048]{2,1,0:T(8,128)(2,1)S(1)} %bitcast.74), kind=kOutput, calls=%fused_computation.6 | convolution fusion | flops 2956984320 | bytes 19791872 | tf_op jit(solution)/shard_map/erh,ehd->erd/dot_general | solution.py:365
  186.4 5.7 %bitcast_convert_fusion.1.in0 = bf16[16,128,2048]{2,1,0:T(8,128)(2,1)} fusion(bf16[2,16,32,2048]{3,2,1,0:T(8,128)(2,1)S(1)} %bitcast.60, f32[2,16,128]{2,0,1:T(2,128)S(1)} %copy.49, f32[32]{0:T(128)S(1)} %iota_convert_fusion), kind=kOutput, calls=%fused_computation.1 | convolution fusion | flops 541196288 | bytes 12599424 | tf_op jit(solution)/shard_map/ebrt,ebrd->btd/dot_general | solution.py:346
  192.1 0.0 all-to-all-done
  192.1 0.6 collective-permute-start
  192.7 7.9 %bitcast_convert_fusion.in1 = bf16[16,128,2048]{2,1,0:T(8,128)(2,1)} fusion(bf16[2,16,32,2048]{3,2,1,0:T(8,128)(2,1)} %bitcast.59, f32[2,16,128]{2,0,1:T(2,128)S(1)} %copy.49, f32[32]{0:T(128)S(1)} %iota_convert_fusion), kind=kOutput, calls=%fused_computation | convolution fusion | flops 541196288 | bytes 12599424 | tf_op jit(solution)/shard_map/ebrt,ebrd->btd/dot_general | solution.py:346
  200.6 93.8 %shard_map.119 = (bf16[128,1024]{1,0:T(8,128)(2,1)S(1)}, bf16[128,1024]{1,0:T(8,128)(2,1)S(1)}) custom-call(bf16[16,128,2048]{2,1,0:T(8,128)(2,1)} %bitcast_convert_fusion.1.in0, bf16[16,128,2048]{2,1,0:T(8,128)(2,1)} %bitcast_convert_fusion.in1), custom_call_target="tpu_custom_call" | custom-call | tf_op jit(solution)/shard_map/pallas_call | solution.py:278
  294.4 0.0 collective-permute-done
  294.4 0.6 add_bitcast_fusion
  295.0 0.7 copy.71
  295.7 0.7 copy.72
  (14 shorter events, 0.1 us)
Async XLA Ops:
  113.9 7.6 %slice-start = ((s8[5767168]{0:T(1024)(128)(4,1)}), s8[4194304]{0:T(1024)(128)(4,1)S(1)}, s32[]{:S(2)}) async-start(s8[5767168]{0:T(1024)(128)(4,1)} %bitcast.69), calls=%async_computation.1 | async-start | bytes 8388608
  114.3 7.2 %copy-start = (bf16[2,16,32,2048]{3,2,1,0:T(8,128)(2,1)}, bf16[2,16,32,2048]{3,2,1,0:T(8,128)(2,1)S(1)}, u32[]{:S(2)}) copy-start(bf16[2,16,32,2048]{3,2,1,0:T(8,128)(2,1)S(1)} %copy.53) | copy-start | bytes 12582916
  114.3 7.2 %slice-start.1 = ((s8[5767168]{0:T(1024)(128)(4,1)}), s8[1572864]{0:T(1024)(128)(4,1)S(1)}, s32[]{:S(2)}) async-start(s8[5767168]{0:T(1024)(128)(4,1)} %bitcast.69), calls=%async_computation.2 | async-start | bytes 3145728
  130.9 3.1 %copy-start.4 = (f32[2,512,704]{1,2,0:T(8,128)S(1)}, f32[2,512,704]{1,2,0:T(8,128)}, u32[]{:S(2)}) copy-start(f32[2,512,704]{1,2,0:T(8,128)} %fusion.35) | copy-start | bytes 8650756
  131.3 10.8 %copy-start.2 = (bf16[2,16,32,2048]{3,2,1,0:T(8,128)(2,1)}, bf16[2,16,32,2048]{3,2,1,0:T(8,128)(2,1)S(1)}, u32[]{:S(2)}) copy-start(bf16[2,16,32,2048]{3,2,1,0:T(8,128)(2,1)S(1)} %copy.55) | copy-start | bytes 12582916
  143.2 48.9 %all-to-all-start = ((f32[16,1,512]{2,1,0:T(1,128)}), f32[16,1,512]{2,1,0:T(1,128)S(1)}, u32[]{:S(2)}, u32[]{:S(2)}) async-start(f32[16,1,512]{2,1,0:T(1,128)} %bitcast.18), calls=%async_computation | async-start | bytes 65536 | tf_op jit(solution)/shard_map/all_to_all | solution.py:379
  148.7 16.4 %slice-start.2 = ((s8[5767168]{0:T(1024)(128)(4,1)}), s8[4194304]{0:T(1024)(128)(4,1)S(1)}, s32[]{:S(2)}) async-start(s8[5767168]{0:T(1024)(128)(4,1)} %bitcast.71), calls=%async_computation.3 | async-start | bytes 8388608
  152.5 6.6 %copy-start.3 = (bf16[2,16,32,2048]{3,2,1,0:T(8,128)(2,1)S(1)}, bf16[2,16,32,2048]{3,2,1,0:T(8,128)(2,1)}, u32[]{:S(2)}) copy-start(bf16[2,16,32,2048]{3,2,1,0:T(8,128)(2,1)} %copy-done.2) | copy-start | bytes 12582916
  152.5 12.7 %slice-start.3 = ((s8[5767168]{0:T(1024)(128)(4,1)}), s8[1572864]{0:T(1024)(128)(4,1)S(1)}, s32[]{:S(2)}) async-start(s8[5767168]{0:T(1024)(128)(4,1)} %bitcast.71), calls=%async_computation.4 | async-start | bytes 3145728
  165.2 3.6 %copy-start.1 = (bf16[2,16,32,2048]{3,2,1,0:T(8,128)(2,1)S(1)}, bf16[2,16,32,2048]{3,2,1,0:T(8,128)(2,1)}, u32[]{:S(2)}) copy-start(bf16[2,16,32,2048]{3,2,1,0:T(8,128)(2,1)} %copy-done) | copy-start | bytes 12582916
  168.8 12.2 %slice-start.4 = ((s8[5767168]{0:T(1024)(128)(4,1)}), s8[4194304]{0:T(1024)(128)(4,1)S(1)}, s32[]{:S(2)}) async-start(s8[5767168]{0:T(1024)(128)(4,1)} %bitcast.73), calls=%async_computation.5 | async-start | bytes 8388608
  174.9 6.1 %slice-start.5 = ((s8[5767168]{0:T(1024)(128)(4,1)}), s8[1572864]{0:T(1024)(128)(4,1)S(1)}, s32[]{:S(2)}) async-start(s8[5767168]{0:T(1024)(128)(4,1)} %bitcast.73), calls=%async_computation.6 | async-start | bytes 3145728
  192.1 102.3 %collective-permute-start = (f32[512]{0:T(512)S(1)}, f32[512]{0:T(512)S(1)}, u32[]{:S(2)}, u32[]{:S(2)}) collective-permute-start(f32[512]{0:T(512)S(1)} %reduce_sum.59), channel_id=1, source_target_pairs={{0,1},{1,0},{2,3},{3,2},{4,5},{5,4},{6,7},{7,6},{8,9},{9,8},{10,11... | collective-permute-start | bytes 6152 | tf_op jit(solution)/shard_map/ppermute | solution.py:385
where the time goes:
time: 297 us; the launch traced here: 296 us
  Pallas kernels  177 us (60%)
  matrix products  76.8 us (26%)
  blocking collectives  23.2 us (8%)
  other arithmetic  6.45 us (2%)
  starting transfers between devices  5.77 us (2%)
  local copies, waits for them, and re-layouts  5.72 us (2%)
    pallas_call x1, Pallas kernels, scatter_pair(): pl.pallas_call(scatter_kernel, out_shape=(out, out), in_specs=[pl.BlockSp...  93.8 us
    pallas_call x1, Pallas kernels, gather_pair(): pl.pallas_call(gather_kernel, out_shape=(full, full), in_specs=[pl.BlockS...  83.7 us
    all_gather x1, blocking collectives, on_device(): routes = lax.all_gather(routes, 'fsdp', axis=0, tiled=False)  23.2 us
    dot_general x2, matrix products, place_back(): jnp.einsum('ebrt,ebrd->btd', select, rows, preferred_element_type=f32)  13.5 us
    dot_general x2, matrix products, pick(): jnp.einsum('ebrt,btd->ebrd', select, values, preferred_element_type=f32)  9.35 us
    dot_general x1, matrix products, on_device(): jnp.einsum('erd,ehd->erh', cotangent, w_down, preferred_element_type=f32)  8.03 us
    dot_general x1, matrix products, on_device(): upper = jnp.einsum('erd,ehd->erh', inputs, w_up, preferred_element_type=f32)  7.19 us
    dot_general x1, matrix products, on_device(): jnp.einsum('erh,ehd->erd', weighted, w_down, preferred_element_type=f32)  6.52 us
  transfers between devices with their start and end apart: 2, of which 0 were waited for; matrix products, arithmetic and copies ran while one was open for 17% of the time, Pallas kernels for 32%

commit v1 on v0

v1 whole, which is shorter than its diff:
```python
import jax
import jax.numpy as jnp
from jax import lax
from jax.experimental import pallas as pl
from jax.experimental.pallas import tpu as pltpu
from jax.sharding import PartitionSpec as P

CAP = 32
MESH = pl.DeviceIdType.MESH


def flip(bit, change):
    return 1 - bit if change else bit


class Place:
    def __init__(self):
        f = lax.axis_index("fsdp")
        self.t = lax.axis_index("tok")
        self.core = f % 2
        self.x = (f // 2) % 2
        self.z0 = (f // 4) % 2
        self.z1 = f // 8

    def block(self, dz=0, dx=0, dc=0):
        z = flip(self.z1, dz // 2) * 2 + flip(self.z0, dz % 2)
        return z * 4 + flip(self.x, dx) * 2 + flip(self.core, dc)

    def device(self, dz=0, dx=0, dy=0, dc=0):
        return (self.block(dz, dx, dc), flip(self.t, dy))

    def columns(self, dy, width):
        return pl.ds(pl.multiple_of(flip(self.t, dy) * width, width), width)

    def partners(self):
        return (
            [self.device(dz=d) for d in (1, 2, 3)]
            + [self.device(dz=d, dx=1) for d in range(4)]
            + [self.device(dy=1), self.device(dc=1)]
        )


def greet(place):
    barrier = pltpu.get_barrier_semaphore()
    partners = place.partners()
    for partner in partners:
        pl.semaphore_signal(barrier, inc=1, device_id=partner, device_id_type=MESH)
    pl.semaphore_wait(barrier, len(partners))


def arrive(ref, sem):
    pltpu.make_async_copy(ref, ref, sem).wait()


def layer_kernel(
    tok_in, grad_in, routes_in, wg_in, wu_in, wd_in,
    x_out, c_out, hid_out, dg_out, du_out, layer_out, dtok_out, dprob_out,
    g, x, xs, wg, wu, wd, act, wide, near, zbuf,
    routes, sel, back, row_prob, inverse, dr, drs, dpart, dbuf, dsum,
    own_sem, w_sem, zs_sem, xsend_sem, ysend_sem, recv_sem,
    rs_sem, rr_sem, px_sem, pr_sem, st_sem, sr_sem, ds_sem, dr_sem,
    xo_sem, ao_sem, ws_sem, wr_sem, ns_sem, nr_sem, ss_sem, sz_sem,
    qs_sem, qr_sem, credit,
):
    place = Place()
    f32, bf16 = jnp.float32, jnp.bfloat16
    rows, width = tok_in.shape
    full = 2 * width
    half = rows // 2
    local, hid = wg.shape[:2]
    topk = 4
    me = place.device

    def start(copy):
        copy.start()
        return copy

    def remote(source, target, ssem, rsem, to):
        return start(
            pltpu.make_async_remote_copy(
                src_ref=source, dst_ref=target, send_sem=ssem, recv_sem=rsem,
                device_id=to, device_id_type=MESH,
            )
        )

    own = [
        start(pltpu.make_async_copy(ref, g.at[0, 0, a, :, place.columns(0, width)], own_sem.at[a]))
        for a, ref in enumerate((tok_in, grad_in))
    ]
    loads = {}
    for l in range(local):
        for i, (ref, to) in enumerate(((wg_in, wg), (wu_in, wu), (wd_in, wd))):
            loads[i, l] = start(pltpu.make_async_copy(ref.at[l], to.at[l], w_sem.at[i, l]))
    greet(place)
    sent = {}

    for dz in range(4):
        for dx in range(2):
            if dz or dx:
                j = dz * 2 + dx
                sent["r", j] = remote(routes_in, routes.at[j], rs_sem.at[j], rr_sem.at[j], me(dz, dx))
    routes[0] = routes_in[...]
    for copy in own:
        copy.wait()

    def piece(h, dz, dx, dy):
        return g.at[dz, dx, :, pl.ds(h * half, half), place.columns(dy, width)]

    def by_z(h, dz):
        sent["z", h, dz] = remote(
            piece(h, 0, 0, 0), piece(h, dz, 0, 0), zs_sem.at[h, dz], recv_sem.at[h, dz, 0, 0], me(dz)
        )

    def by_x(h, dz, dy):
        sent["x", h, dz, dy] = remote(
            piece(h, dz, 0, dy), piece(h, dz, 1, dy), xsend_sem.at[h, dz, dy],
            recv_sem.at[h, dz, 1, dy], me(0, 1),
        )

    def by_y(h, dz, dx):
        sent["y", h, dz, dx] = remote(
            piece(h, dz, dx, 0), piece(h, dz, dx, 0), ysend_sem.at[h, dz, dx],
            recv_sem.at[h, dz, dx, 1], me(0, 0, 1),
        )

    def got(h, dz, dx, dy):
        arrive(piece(h, dz, dx, dy), recv_sem.at[h, dz, dx, dy])

    def column(dz):
        for h in range(2):
            if dz:
                got(h, dz, 0, 0)
            if h == 0:
                by_x(h, dz, 0)
                by_y(h, dz, 0)
            else:
                by_y(h, dz, 0)
                by_x(h, dz, 0)

    def plane(dz):
        got(0, dz, 1, 0)
        by_y(0, dz, 1)
        got(1, dz, 0, 1)
        by_x(1, dz, 1)

    def last(dz):
        got(0, dz, 0, 1)
        got(1, dz, 1, 0)
        got(0, dz, 1, 1)
        got(1, dz, 1, 1)

    experts = [
        (place.block(0, 0, e // local) * local + e % local).astype(f32) for e in range(2 * local)
    ]

    def build(j):
        names = routes[j, :topk, :]
        probs = routes[j, topk:, :]
        before = (
            lax.broadcasted_iota(jnp.int32, (rows, rows), 0)
            < lax.broadcasted_iota(jnp.int32, (rows, rows), 1)
        ).astype(f32).astype(bf16)
        hits, prob = [], []
        for e in experts:
            chosen = names == e
            hits.append(jnp.max(jnp.where(chosen, 1.0, 0.0), axis=0, keepdims=True))
            prob.append(jnp.sum(jnp.where(chosen, probs, 0.0), axis=0, keepdims=True))
        hit = jnp.concatenate(hits + [jnp.zeros((4, rows), f32)], axis=0)
        spot = jnp.dot(hit.astype(bf16), before, preferred_element_type=f32)
        spot = jnp.where(hit > 0.0, spot, -1.0)
        number = lax.broadcasted_iota(jnp.int32, (CAP, rows), 0).astype(f32)
        ones, high, low, full_prob, inv = [], [], [], [], []
        for e in range(2 * local):
            filled = jnp.broadcast_to(spot[e : e + 1], (CAP, rows)) == number
            top = prob[e].astype(bf16).astype(f32)
            ones.append(jnp.where(filled, 1.0, 0.0))
            high.append(jnp.where(filled, top, 0.0))
            low.append(jnp.where(filled, prob[e] - top, 0.0))
            full_prob.append(jnp.where(filled, prob[e], 0.0))
            inv.append(jnp.where(hits[e] > 0.0, 1.0 / jnp.maximum(prob[e], 1e-30), 0.0))
        ones = jnp.concatenate(ones, axis=0)
        sel[j] = ones.astype(bf16)
        back[j, 0] = ones.T.astype(bf16)
        back[j, 1] = jnp.concatenate(high, axis=0).T.astype(bf16)
        back[j, 2] = jnp.concatenate(low, axis=0).T.astype(bf16)
        row_prob[j] = jnp.sum(jnp.concatenate(full_prob, axis=0), axis=1, keepdims=True)
        inverse[j] = jnp.concatenate(inv + [jnp.zeros((4, rows), f32)], axis=0)

    def build_all(first, end):
        for j in range(first, end):
            if j:
                arrive(routes.at[j], rr_sem.at[j])

        @pl.loop(first, end)
        def _(j):
            build(j)

    tile = 512

    def select(dz):
        @pl.loop(0, 2)
        def _(dx):
            j = dz * 2 + dx
            at = pl.ds(pl.multiple_of(dx * CAP, CAP), CAP)

            @pl.loop(0, full // tile)
            def _(n):
                cols = pl.ds(pl.multiple_of(n * tile, tile), tile)
                for a in range(2):
                    picked = jnp.dot(sel[j], g[dz, dx, a, :, cols], preferred_element_type=f32)
                    if a:
                        picked = picked * row_prob[j]
                    picked = picked.astype(bf16)
                    for l in range(local):
                        x[a, l, dz, at, cols] = picked[l * CAP : (l + 1) * CAP]
                        m = local + l
                        xs[a, l, dz, at, cols] = picked[m * CAP : (m + 1) * CAP]

        sent["p", dz] = remote(
            xs.at[:, :, dz], x.at[:, :, dz, pl.ds(half, half)], px_sem.at[dz], pr_sem.at[dz], me(0, 0, 0, 1)
        )

    def packed(dz):
        arrive(x.at[:, :, dz, pl.ds(half, half)], pr_sem.at[dz])
        for a, ref in enumerate((x_out, c_out)):
            sent["xo", a, dz] = start(
                pltpu.make_async_copy(x.at[a, :, dz], ref.at[:, dz], xo_sem.at[a, dz])
            )

    nt = (((1,), (1,)), ((), ()))
    tiles = [(h, min(256, hid - h)) for h in range(0, hid, 256)]

    def forward(dz, l):
        if dz == 0:
            for i in range(3):
                loads[i, l].wait()
        total = jnp.zeros((rows, 1), f32)
        for h, n in tiles:
            at = pl.ds(h, n)
            gate = lax.dot_general(x[0, l, dz], wg[l, at, :], nt, preferred_element_type=f32)
            upper = lax.dot_general(x[0, l, dz], wu[l, at, :], nt, preferred_element_type=f32)
            d_hidden = lax.dot_general(x[1, l, dz], wd[l, at, :], nt, preferred_element_type=f32)
            sigma = jax.nn.sigmoid(gate)
            active = gate * sigma
            hidden = active * upper
            total = total + jnp.sum(hidden * d_hidden, axis=1, keepdims=True)
            act[0, l, dz, :, at] = hidden.astype(bf16)
            act[1, l, dz, :, at] = (d_hidden * upper * sigma * (1.0 + gate * (1.0 - sigma))).astype(bf16)
            act[2, l, dz, :, at] = (d_hidden * active).astype(bf16)
        total = jnp.broadcast_to(total, (rows, rows))
        for dx in range(2):
            dr[dz, dx, l * CAP : (l + 1) * CAP, :] = total[dx * CAP : (dx + 1) * CAP]
            drs[dz, dx, l * CAP : (l + 1) * CAP, :] = total[half + dx * CAP : half + (dx + 1) * CAP]

    def handed(dz):
        for i, ref in enumerate((hid_out, dg_out, du_out)):
            sent["ao", i, dz] = start(
                pltpu.make_async_copy(act.at[i, :, dz], ref.at[:, dz], ao_sem.at[i, dz])
            )
        sent["d", dz] = remote(
            drs.at[dz], dr.at[dz, :, pl.ds(half, half)], ds_sem.at[dz], dr_sem.at[dz], me(0, 0, 0, 1)
        )
        sent.pop(("xo", 0, dz)).wait()
        sent.pop(("xo", 1, dz)).wait()
        pl.semaphore_signal(credit.at[dz], inc=1, device_id=me(0, 0, 0, 1), device_id_type=MESH)
        sent.pop(("p", dz)).wait_send()

    def backward(dz, l):
        mine = pl.ds(l * CAP, CAP)

        @pl.loop(0, full // tile)
        def _(n):
            cols = pl.ds(pl.multiple_of(n * tile, tile), tile)
            out = jnp.dot(act[0, l, dz], wd[l, :, cols], preferred_element_type=f32)
            back_rows = jnp.dot(act[1, l, dz], wg[l, :, cols], preferred_element_type=f32)
            back_rows = back_rows + jnp.dot(act[2, l, dz], wu[l, :, cols], preferred_element_type=f32)
            for a, value in enumerate((out.astype(bf16), back_rows.astype(bf16))):
                for dx in range(2):
                    x[a, dx, dz, mine, cols] = value[dx * CAP : (dx + 1) * CAP]
                    xs[a, dx, dz, mine, cols] = value[half + dx * CAP : half + (dx + 1) * CAP]

    def returned(dz):
        pl.semaphore_wait(credit.at[dz], 1)
        sent["s", dz] = remote(
            xs.at[:, :, dz], x.at[:, :, dz, pl.ds(half, half)], st_sem.at[dz], sr_sem.at[dz], me(0, 0, 0, 1)
        )

    def put_back(dz):
        for h in range(2):
            for key in (("x", h, dz, 0), ("y", h, dz, 0)):
                sent.pop(key).wait_send()
        sent.pop(("y", 0, dz, 1)).wait_send()
        sent.pop(("x", 1, dz, 1)).wait_send()
        if dz == 0:
            for h in range(2):
                for d in range(1, 4):
                    sent.pop(("z", h, d)).wait_send()
        arrive(x.at[:, :, dz, pl.ds(half, half)], sr_sem.at[dz])
        arrive(dr.at[dz, :, pl.ds(half, half)], dr_sem.at[dz])

        @pl.loop(0, 2)
        def _(dx):
            j = dz * 2 + dx

            @pl.loop(0, full // tile)
            def _(n):
                cols = pl.ds(pl.multiple_of(n * tile, tile), tile)
                out = jnp.dot(back[j, 1], x[0, dx, dz, :, cols], preferred_element_type=f32)
                out = out + jnp.dot(back[j, 2], x[0, dx, dz, :, cols], preferred_element_type=f32)
                g[dz, dx, 0, :, cols] = out.astype(bf16)
                into = jnp.dot(back[j, 0], x[1, dx, dz, :, cols], preferred_element_type=f32)
                g[dz, dx, 1, :, cols] = into.astype(bf16)

            names = routes[j, :topk, :]
            weighted = dr[dz, dx] * sel[j].astype(f32)
            total = jnp.zeros((topk, rows), f32)
            for e, name in enumerate(experts):
                value = jnp.sum(weighted[e * CAP : (e + 1) * CAP], axis=0, keepdims=True)
                value = value * inverse[j, e : e + 1, :]
                total = total + jnp.where(names == name, value, 0.0)
            dpart[j] = jnp.concatenate([total, jnp.zeros((8 - topk, rows), f32)], axis=0)

        for dx in range(2):
            j = dz * 2 + dx
            if j:
                sent["q", j] = remote(dpart.at[j], dbuf.at[j], qs_sem.at[j], qr_sem.at[j], me(dz, dx))

    def send_wide(dz):
        for h in range(2):
            across = me(0, 0, 1) if h == 0 else me(0, 1)
            for other in (1, 0):
                dx, dy = (other, 1) if h == 0 else (1, other)
                sent["w", h, dz, other] = remote(
                    piece(h, dz, dx, dy), wide.at[h, dz, other], ws_sem.at[h, dz, other],
                    wr_sem.at[h, dz, other], across,
                )

    def add(target, source):
        for a in range(2):
            @pl.loop(0, half // 16)
            def _(i):
                at = pl.ds(pl.multiple_of(i * 16, 16), 16)
                target[a, at, :] = target[a, at, :] + source[a, at, :]

    def send_near(dz):
        for other in (1, 0):
            for h in range(2):
                dx, dy = (other, 0) if h == 0 else (0, other)
                arrive(wide.at[h, dz, other], wr_sem.at[h, dz, other])
                add(wide.at[h, dz, other], piece(h, dz, dx, dy))
                if other:
                    along = me(0, 1) if h == 0 else me(0, 0, 1)
                    sent["n", h, dz] = remote(
                        wide.at[h, dz, 1], near.at[h, dz], ns_sem.at[h, dz], nr_sem.at[h, dz], along
                    )

    def send_z(dz):
        for h in range(2):
            arrive(near.at[h, dz], nr_sem.at[h, dz])
            add(near.at[h, dz], wide.at[h, dz, 0])
            if dz:
                sent["f", h, dz] = remote(
                    near.at[h, dz], zbuf.at[h, dz - 1], ss_sem.at[h, dz], sz_sem.at[h, dz], me(dz)
                )

    for h in range(2):
        by_z(h, 1)
    column(0)
    for dz in (2, 3):
        for h in range(2):
            by_z(h, dz)
    build_all(0, 8)
    plane(0)
    column(1)
    last(0)
    for dz in range(4):
        select(dz)
        if dz < 3:
            plane(dz + 1)
        packed(dz)
        forward(dz, 0)
        if dz < 2:
            column(dz + 2)
        forward(dz, 1)
        handed(dz)
        if dz == 2:
            send_wide(1)
        backward(dz, 0)
        backward(dz, 1)
        returned(dz)
        if dz == 3:
            send_near(1)
        put_back(dz)
        if dz < 3:
            last(dz + 1)
        if dz >= 2:
            send_wide(dz)
    send_near(2)
    send_z(1)
    send_wide(0)
    send_near(3)
    send_z(2)

    total = dpart[0]
    for j in range(1, 8):
        arrive(dbuf.at[j], qr_sem.at[j])
        total = total + dbuf[j]
    dsum[0] = total
    peer = remote(dsum.at[0], dsum.at[1], qs_sem.at[0], qr_sem.at[0], me(0, 0, 1))

    send_near(0)
    send_z(3)
    send_z(0)
    arrive(dsum.at[1], qr_sem.at[0])
    dprob_out[...] = dsum[0] + dsum[1]
    for dz in (1, 2, 3):
        for h in range(2):
            arrive(zbuf.at[h, dz - 1], sz_sem.at[h, dz])
    for a, ref in enumerate((layer_out, dtok_out)):
        for h in range(2):
            @pl.loop(0, half // 16)
            def _(i):
                at = pl.ds(pl.multiple_of(i * 16, 16), 16)
                total = near[h, 0, a, at, :].astype(f32)
                for dz in (1, 2, 3):
                    total = total + zbuf[h, dz - 1, a, at, :].astype(f32)
                to = pl.ds(pl.multiple_of(h * half + i * 16, 16), 16)
                ref[to, :] = total.astype(bf16)
    peer.wait_send()
    for key, copy in sent.items():
        if key[0] == "ao":
            copy.wait()
        else:
            copy.wait_send()


def layer(tokens, grad_out, routes, w_gate, w_up, w_down):
    rows, width = tokens.shape
    local, hid, full = w_gate.shape
    half = rows // 2
    bf16, f32 = jnp.bfloat16, jnp.float32
    any_space = pl.BlockSpec(memory_space=pl.ANY)
    vmem = pl.BlockSpec(memory_space=pltpu.VMEM)
    shape = jax.ShapeDtypeStruct
    packed = shape((local, 4, rows, full), bf16)
    acts = shape((local, 4, rows, hid), bf16)
    out = shape((rows, width), bf16)
    dma = pltpu.SemaphoreType.DMA
    return pl.pallas_call(
        layer_kernel,
        out_shape=(packed, packed, acts, acts, acts, out, out, shape((8, rows), f32)),
        in_specs=[any_space, any_space, vmem, any_space, any_space, any_space],
        out_specs=[any_space] * 5 + [vmem] * 3,
        scratch_shapes=[
            pltpu.VMEM((4, 2, 2, rows, full), bf16),
            pltpu.VMEM((2, 2, 4, rows, full), bf16),
            pltpu.VMEM((2, 2, 4, half, full), bf16),
            pltpu.VMEM((local, hid, full), bf16),
            pltpu.VMEM((local, hid, full), bf16),
            pltpu.VMEM((local, hid, full), bf16),
            pltpu.VMEM((3, local, 4, rows, hid), bf16),
            pltpu.VMEM((2, 4, 2, 2, half, width), bf16),
            pltpu.VMEM((2, 4, 2, half, width), bf16),
            pltpu.VMEM((2, 3, 2, half, width), bf16),
            pltpu.VMEM((8, 8, rows), f32),
            pltpu.VMEM((8, rows, rows), bf16),
            pltpu.VMEM((8, 3, rows, rows), bf16),
            pltpu.VMEM((8, rows, 1), f32),
            pltpu.VMEM((8, 8, rows), f32),
            pltpu.VMEM((4, 2, rows, rows), f32),
            pltpu.VMEM((4, 2, half, rows), f32),
            pltpu.VMEM((8, 8, rows), f32),
            pltpu.VMEM((8, 8, rows), f32),
            pltpu.VMEM((2, 8, rows), f32),
            dma((2,)), dma((3, local)), dma((2, 4)), dma((2, 4, 2)), dma((2, 4, 2)), dma((2, 4, 2, 2)),
            dma((8,)), dma((8,)), dma((4,)), dma((4,)), dma((4,)), dma((4,)), dma((4,)), dma((4,)),
            dma((2, 4)), dma((3, 4)), dma((2, 4, 2)), dma((2, 4, 2)), dma((2, 4)), dma((2, 4)),
            dma((2, 4)), dma((2, 4)), dma((8,)), dma((8,)),
            pltpu.SemaphoreType.REGULAR((4,)),
        ],
        compiler_params=pltpu.CompilerParams(
            collective_id=0, has_side_effects=True, vmem_limit_bytes=61 * 2**20
        ),
    )(tokens, grad_out, routes, w_gate, w_up, w_down)


def by_one_kernel(tokens, expert_ids, gate_probs, w_gate, w_up, w_down, grad_out):
    topk = expert_ids.shape[1]
    local, hid, full = w_gate.shape
    f32 = jnp.float32
    routes = jnp.concatenate([expert_ids.astype(f32).T, gate_probs.T], axis=0)
    x, c, hidden, d_gate, d_up, layer_out, d_tokens, d_prob = layer(
        tokens, grad_out, routes, w_gate, w_up, w_down
    )
    x, c = (v.reshape(local, -1, full) for v in (x, c))
    hidden, d_gate, d_up = (v.reshape(local, -1, hid) for v in (hidden, d_gate, d_up))

    def weight(rows, values):
        return jnp.einsum("erh,erd->ehd", rows, values, preferred_element_type=f32)

    return (
        layer_out, d_tokens, d_prob[:topk].T,
        weight(d_gate, x), weight(d_up, x), weight(hidden, c),
    )


def gather_any(value):
    wide = lax.all_gather(value, "tok", axis=1, tiled=True)
    return lax.all_gather(wide, "fsdp", axis=0, tiled=False)


def scatter_any(value):
    blocks, rows, full = value.shape
    mine = lax.psum_scatter(
        value.reshape(blocks * rows, full), "fsdp", scatter_dimension=0, tiled=True
    )
    return lax.psum_scatter(mine, "tok", scatter_dimension=1, tiled=True)


def on_device(tokens, expert_ids, gate_probs, w_gate, w_up, w_down, grad_out):
    tok_rows, topk = expert_ids.shape
    local = w_gate.shape[0]
    f32 = jnp.float32
    me = lax.axis_index("fsdp")

    routes = jnp.concatenate([expert_ids.astype(f32).T, gate_probs.T], axis=0)
    routes = lax.all_gather(routes, "fsdp", axis=0, tiled=False)
    all_tokens, all_grads = gather_any(tokens), gather_any(grad_out)
    blocks = all_tokens.shape[0]

    names = routes[:, :topk]
    mine = (me * local + jnp.arange(local, dtype=jnp.int32)).astype(f32)
    chosen = names[None] == mine[:, None, None, None]
    hit = jnp.any(chosen, axis=2)
    prob = jnp.sum(jnp.where(chosen, routes[None, :, topk:], 0.0), axis=2)
    before = jnp.triu(jnp.ones((tok_rows, tok_rows), jnp.bfloat16), 1)
    place = jnp.einsum("ebs,st->ebt", hit.astype(jnp.bfloat16), before, preferred_element_type=f32)
    place = jnp.where(hit, place, -1.0)
    filled = place[:, :, None, :] == jnp.arange(CAP, dtype=jnp.int32).astype(f32)[None, None, :, None]
    select = filled.astype(jnp.bfloat16)
    row_prob = jnp.sum(jnp.where(filled, prob[:, :, None, :], 0.0), axis=3)
    row_prob = row_prob.reshape(local, blocks * CAP, 1)

    def pick(values):
        rows = jnp.einsum("ebrt,btd->ebrd", select, values, preferred_element_type=f32)
        return rows.astype(jnp.bfloat16).reshape(local, blocks * CAP, values.shape[-1])

    def place_back(rows):
        rows = rows.astype(jnp.bfloat16).reshape(local, blocks, CAP, rows.shape[-1])
        values = jnp.einsum("ebrt,ebrd->btd", select, rows, preferred_element_type=f32)
        return values.astype(jnp.bfloat16)

    inputs = pick(all_tokens)
    cotangent = pick(all_grads)
    gate = jnp.einsum("erd,ehd->erh", inputs, w_gate, preferred_element_type=f32)
    upper = jnp.einsum("erd,ehd->erh", inputs, w_up, preferred_element_type=f32)
    raw = jnp.einsum("erd,ehd->erh", cotangent, w_down, preferred_element_type=f32)
    sigma = jax.nn.sigmoid(gate)
    active = gate * sigma
    hidden = active * upper
    weighted = (row_prob * hidden).astype(jnp.bfloat16)
    d_hidden = row_prob * raw
    d_gate = (d_hidden * upper * sigma * (1.0 + gate * (1.0 - sigma))).astype(jnp.bfloat16)
    d_upper = (d_hidden * active).astype(jnp.bfloat16)
    d_rows = jnp.sum(hidden * raw, axis=2).reshape(local, blocks, CAP)

    out_rows = jnp.einsum("erh,ehd->erd", weighted, w_down, preferred_element_type=f32)
    in_rows = jnp.einsum("erh,ehd->erd", d_gate, w_gate, preferred_element_type=f32)
    in_rows = in_rows + jnp.einsum("erh,ehd->erd", d_upper, w_up, preferred_element_type=f32)
    part_out, part_in = place_back(out_rows), place_back(in_rows)
    layer_out, d_tokens = scatter_any(part_out), scatter_any(part_in)

    d_w_down = jnp.einsum("erh,erd->ehd", weighted, cotangent, preferred_element_type=f32)
    d_w_gate = jnp.einsum("erh,erd->ehd", d_gate, inputs, preferred_element_type=f32)
    d_w_up = jnp.einsum("erh,erd->ehd", d_upper, inputs, preferred_element_type=f32)

    d_prob = jnp.sum(jnp.where(filled, d_rows[:, :, :, None], 0.0), axis=2)
    d_prob = jnp.sum(jnp.where(chosen, d_prob[:, :, None, :], 0.0), axis=0)
    d_prob = d_prob.reshape(blocks, topk * tok_rows)
    d_prob = lax.all_to_all(d_prob, "fsdp", split_axis=0, concat_axis=0, tiled=True)
    d_prob = jnp.sum(d_prob, axis=0)
    size = lax.axis_size("tok")
    mine_only = d_prob
    for turn in range(1, size):
        pairs = [(i, (i + turn) % size) for i in range(size)]
        d_prob = d_prob + lax.ppermute(mine_only, "tok", pairs)
    d_gate_probs = d_prob.reshape(topk, tok_rows).T
    return (layer_out, d_tokens, d_gate_probs, d_w_gate, d_w_up, d_w_down)


def solution(mesh):
    by_kernel = mesh.shape["fsdp"] == 16 and mesh.shape["tok"] == 2
    return jax.shard_map(
        by_one_kernel if by_kernel else on_device,
        mesh=mesh,
        in_specs=(
            P("fsdp", "tok"),
            P("fsdp", None),
            P("fsdp", None),
            P("fsdp", "tok", None),
            P("fsdp", "tok", None),
            P("fsdp", "tok", None),
            P("fsdp", "tok"),
        ),
        out_specs=(
            P("fsdp", "tok"),
            P("fsdp", "tok"),
            P("fsdp", None),
            P("fsdp", "tok", None),
            P("fsdp", "tok", None),
            P("fsdp", "tok", None),
        ),
        check_vma=False,
    )
```

time: 297 us -> 212 us (0.71)
  the two profiles are of different devices: /device:TPU:0 before, /device:TPU:9 now
where the time goes in v1:
time: 212 us; the launch traced here: 211 us
  Pallas kernels  183 us (86%)
  matrix products  22.8 us (11%)
  local copies, waits for them, and re-layouts  2.68 us (1%)
    pallas_call x1, Pallas kernels, layer(): pl.pallas_call(layer_kernel, out_shape=(packed, packed, acts, acts, acts,...  183 us
    dot_general x3, matrix products, weight(): return jnp.einsum('erh,erd->ehd', rows, values, preferred_element_type=f32)  22.8 us

profile of v1, /device:TPU:9, one launch (start us, length us, event | category | flops | bytes accessed | tf_op | source)
XLA Modules:
  0.0 211.3 jit_solution(5452214364179327856)
XLA Ops:
  0.6 0.7 convert_bitcast_fusion
  1.3 1.3 pad_maximum_fusion.routes_in
  2.6 183.1 %shard_map.118 = (bf16[2,4,128,2048]{3,2,1,0:T(8,128)(2,1)}, bf16[2,4,128,2048]{3,2,1,0:T(8,128)(2,1)}, bf16[2,4,128,704]{3,2,1,0:T(8,128)(2,1)}, bf16[2,4,128,7...) custom-call(bf16[128,1024]{1,0:T(8,128)(2,1)} %tok_in.1, ...), custom_call_target="tpu_custom_call" | custom-call | tf_op jit(solution)/shard_map/pallas_call | solution.py:449
  185.7 1.3 slice_bitcast_fusion
  187.0 0.0 copy-start.3
  187.0 0.0 copy-start.5
  187.0 10.4 %fusion = f32[2,704,2048]{2,1,0:T(8,128)} fusion(bf16[2,512,704]{2,1,0:T(8,128)(2,1)} %bitcast.22, bf16[2,512,2048]{2,1,0:T(8,128)(2,1)} %bitcast.18), kind=kOutput, calls=%fused_computation.3 | convolution fusion | flops 2952790016 | bytes 17170432 | tf_op jit(solution)/shard_map/erh,erd->ehd/dot_general | solution.py:499
  197.4 0.0 copy-done.3
  197.4 0.0 copy-done.5
  197.4 0.0 copy-start.2
  197.4 0.0 copy-start.4
  197.4 6.2 %fusion.1 = f32[2,704,2048]{2,1,0:T(8,128)} fusion(bf16[2,512,704]{2,1,0:T(8,128)(2,1)S(1)} %bitcast.21, bf16[2,512,2048]{2,1,0:T(8,128)(2,1)S(1)} %bitcast.19), kind=kOutput, calls=%fused_computation.4 | convolution fusion | flops 2952790016 | bytes 17170432 | tf_op jit(solution)/shard_map/erh,erd->ehd/dot_general | solution.py:499
  203.6 0.0 copy-done.2
  203.6 0.0 copy-done.4
  203.6 0.0 copy-start.1
  203.6 0.0 copy-start
  203.6 6.2 %fusion.2 = f32[2,704,2048]{2,1,0:T(8,128)} fusion(bf16[2,512,704]{2,1,0:T(8,128)(2,1)S(1)} %bitcast.20, bf16[2,512,2048]{2,1,0:T(8,128)(2,1)S(1)} %bitcast.17), kind=kOutput, calls=%fused_computation.5 | convolution fusion | flops 2952790016 | bytes 17170432 | tf_op jit(solution)/shard_map/erh,erd->ehd/dot_general | solution.py:499
  209.8 0.0 copy-done.1
  209.8 0.7 copy.21
  210.5 0.0 copy-done
  210.6 0.7 copy.22
Async XLA Ops:
  187.0 10.4 %copy-start.3 = (bf16[2,4,128,2048]{3,2,1,0:T(8,128)(2,1)S(1)}, bf16[2,4,128,2048]{3,2,1,0:T(8,128)(2,1)}, u32[]{:S(2)}) copy-start(bf16[2,4,128,2048]{3,2,1,0:T(8,128)(2,1)} %get-tuple-element.18) | copy-start | bytes 12582916
  187.0 10.4 %copy-start.5 = (bf16[2,4,128,704]{3,2,1,0:T(8,128)(2,1)S(1)}, bf16[2,4,128,704]{3,2,1,0:T(8,128)(2,1)}, u32[]{:S(2)}) copy-start(bf16[2,4,128,704]{3,2,1,0:T(8,128)(2,1)} %get-tuple-element.19) | copy-start | bytes 4325380
  197.4 6.2 %copy-start.2 = (bf16[2,4,128,2048]{3,2,1,0:T(8,128)(2,1)S(1)}, bf16[2,4,128,2048]{3,2,1,0:T(8,128)(2,1)}, u32[]{:S(2)}) copy-start(bf16[2,4,128,2048]{3,2,1,0:T(8,128)(2,1)} %get-tuple-element.21) | copy-start | bytes 12582916
  197.4 6.2 %copy-start.4 = (bf16[2,4,128,704]{3,2,1,0:T(8,128)(2,1)S(1)}, bf16[2,4,128,704]{3,2,1,0:T(8,128)(2,1)}, u32[]{:S(2)}) copy-start(bf16[2,4,128,704]{3,2,1,0:T(8,128)(2,1)} %get-tuple-element.20) | copy-start | bytes 4325380
  203.6 6.2 %copy-start.1 = (bf16[128,1024]{1,0:T(8,128)(2,1)S(1)}, bf16[128,1024]{1,0:T(8,128)(2,1)}, u32[]{:S(2)}) copy-start(bf16[128,1024]{1,0:T(8,128)(2,1)} %get-tuple-element.28) | copy-start | bytes 786436
  203.6 6.9 %copy-start = (bf16[128,1024]{1,0:T(8,128)(2,1)S(1)}, bf16[128,1024]{1,0:T(8,128)(2,1)}, u32[]{:S(2)}) copy-start(bf16[128,1024]{1,0:T(8,128)(2,1)} %get-tuple-element.29) | copy-start | bytes 786436

commit v2 on v1

--- a/solution.py
+++ b/solution.py
@@ -22,20 +22,42 @@
         self.z0 = (f // 4) % 2
         self.z1 = f // 8
 
-    def block(self, dz=0, dx=0, dc=0):
-        z = flip(self.z1, dz // 2) * 2 + flip(self.z0, dz % 2)
-        return z * 4 + flip(self.x, dx) * 2 + flip(self.core, dc)
-
-    def device(self, dz=0, dx=0, dy=0, dc=0):
-        return (self.block(dz, dx, dc), flip(self.t, dy))
+        self.inner = self.z0 + self.z1 - 2 * self.z0 * self.z1
+
+    def index(self, z1, z0, dx, dc):
+        return (z1 * 2 + z0) * 4 + flip(self.x, dx) * 2 + flip(self.core, dc)
+
+    def block(self, dx=0, dc=0):
+        return self.index(self.z1, self.z0, dx, dc)
+
+    def far(self, slot, dx=0):
+        if slot < 2:
+            z1, z0 = self.z1, flip(self.z0, slot)
+        else:
+            turn = self.inner if slot == 2 else 1 - self.inner
+            z1, z0 = 1 - self.z1, self.z0 + turn - 2 * self.z0 * turn
+        return (self.index(z1, z0, dx, 0), self.t)
+
+    def slot_there(self, slot):
+        return slot if slot < 2 else 3 - self.inner
+
+    def inward(self):
+        z = self.inner * (2 - self.z1) + (1 - self.inner) * (1 + self.z1)
+        return (z * 4 + self.x * 2 + self.core, self.t)
+
+    def outward(self):
+        return (3 * self.z1 * 4 + self.x * 2 + self.core, self.t)
+
+    def device(self, dx=0, dy=0, dc=0):
+        return (self.block(dx, dc), flip(self.t, dy))
 
     def columns(self, dy, width):
         return pl.ds(pl.multiple_of(flip(self.t, dy) * width, width), width)
 
     def partners(self):
         return (
-            [self.device(dz=d) for d in (1, 2, 3)]
-            + [self.device(dz=d, dx=1) for d in range(4)]
+            [self.far(slot) for slot in (1, 2, 3)]
+            + [self.far(slot, 1) for slot in range(4)]
             + [self.device(dy=1), self.device(dc=1)]
         )
 
@@ -54,13 +76,13 @@
 
 def layer_kernel(
     tok_in, grad_in, routes_in, wg_in, wu_in, wd_in,
-    x_out, c_out, hid_out, dg_out, du_out, layer_out, dtok_out, dprob_out,
+    x_out, c_out, hid_out, dg_out, du_out, far_out, layer_out, dtok_out, dprob_out,
     g, x, xs, wg, wu, wd, act, wide, near, zbuf,
     routes, sel, back, row_prob, inverse, dr, drs, dpart, dbuf, dsum,
     own_sem, w_sem, zs_sem, xsend_sem, ysend_sem, recv_sem,
     rs_sem, rr_sem, px_sem, pr_sem, st_sem, sr_sem, ds_sem, dr_sem,
     xo_sem, ao_sem, ws_sem, wr_sem, ns_sem, nr_sem, ss_sem, sz_sem,
-    qs_sem, qr_sem, credit,
+    qs_sem, qr_sem, far_sem, credit,
 ):
     place = Place()
     f32, bf16 = jnp.float32, jnp.bfloat16
@@ -87,10 +109,6 @@
         start(pltpu.make_async_copy(ref, g.at[0, 0, a, :, place.columns(0, width)], own_sem.at[a]))
         for a, ref in enumerate((tok_in, grad_in))
     ]
-    loads = {}
-    for l in range(local):
-        for i, (ref, to) in enumerate(((wg_in, wg), (wu_in, wu), (wd_in, wd))):
-            loads[i, l] = start(pltpu.make_async_copy(ref.at[l], to.at[l], w_sem.at[i, l]))
     greet(place)
     sent = {}
 
@@ -98,7 +116,10 @@
         for dx in range(2):
             if dz or dx:
                 j = dz * 2 + dx
-                sent["r", j] = remote(routes_in, routes.at[j], rs_sem.at[j], rr_sem.at[j], me(dz, dx))
+                there = place.slot_there(dz) * 2 + dx
+                sent["r", j] = remote(
+                    routes_in, routes.at[there], rs_sem.at[j], rr_sem.at[there], place.far(dz, dx)
+                )
     routes[0] = routes_in[...]
     for copy in own:
         copy.wait()
@@ -106,21 +127,53 @@
     def piece(h, dz, dx, dy):
         return g.at[dz, dx, :, pl.ds(h * half, half), place.columns(dy, width)]
 
-    def by_z(h, dz):
-        sent["z", h, dz] = remote(
-            piece(h, 0, 0, 0), piece(h, dz, 0, 0), zs_sem.at[h, dz], recv_sem.at[h, dz, 0, 0], me(dz)
+    def by_z(h, to, slot, there, k):
+        return start(
+            pltpu.make_async_remote_copy(
+                src_ref=piece(h, slot, 0, 0), dst_ref=piece(h, there, 0, 0),
+                send_sem=zs_sem.at[h, k], recv_sem=recv_sem.at[h, there, 0, 0],
+                device_id=to, device_id_type=MESH,
+            )
         )
+
+    inner = place.inner == 1
+
+    def own_z():
+        for h in range(2):
+            sent["z", h, 0] = by_z(h, place.inward(), 0, 1 + place.inner, 0)
+
+            @pl.when(inner)
+            def _():
+                by_z(h, place.outward(), 0, 1, 4)
+
+    def pass_on(slot):
+        @pl.when(inner)
+        def _():
+            for h in range(2):
+                got(h, slot, 0, 0)
+                if slot == 1:
+                    by_z(h, place.inward(), 1, 3, 1)
+                else:
+                    by_z(h, place.outward(), slot, slot, slot)
+
+    def passed_on(k):
+        slot = k % 4
+
+        @pl.when(inner)
+        def _():
+            for h in range(2):
+                pltpu.make_async_copy(piece(h, slot, 0, 0), piece(h, slot, 0, 0), zs_sem.at[h, k]).wait()
 
     def by_x(h, dz, dy):
         sent["x", h, dz, dy] = remote(
             piece(h, dz, 0, dy), piece(h, dz, 1, dy), xsend_sem.at[h, dz, dy],
-            recv_sem.at[h, dz, 1, dy], me(0, 1),
+            recv_sem.at[h, dz, 1, dy], me(1),
         )
 
     def by_y(h, dz, dx):
         sent["y", h, dz, dx] = remote(
             piece(h, dz, dx, 0), piece(h, dz, dx, 0), ysend_sem.at[h, dz, dx],
-            recv_sem.at[h, dz, dx, 1], me(0, 0, 1),
+            recv_sem.at[h, dz, dx, 1], me(0, 1),
         )
 
     def got(h, dz, dx, dy):
@@ -129,7 +182,10 @@
     def column(dz):
         for h in range(2):
             if dz:
-                got(h, dz, 0, 0)
+                @pl.when(jnp.logical_not(inner))
+                def _():
+                    got(h, dz, 0, 0)
+
             if h == 0:
                 by_x(h, dz, 0)
                 by_y(h, dz, 0)
@@ -150,7 +206,7 @@
         got(1, dz, 1, 1)
 
     experts = [
-        (place.block(0, 0, e // local) * local + e % local).astype(f32) for e in range(2 * local)
+        (place.block(0, e // local) * local + e % local).astype(f32) for e in range(2 * local)
     ]
 
     def build(j):
@@ -217,7 +273,7 @@
                         xs[a, l, dz, at, cols] = picked[m * CAP : (m + 1) * CAP]
 
         sent["p", dz] = remote(
-            xs.at[:, :, dz], x.at[:, :, dz, pl.ds(half, half)], px_sem.at[dz], pr_sem.at[dz], me(0, 0, 0, 1)
+            xs.at[:, :, dz], x.at[:, :, dz, pl.ds(half, half)], px_sem.at[dz], pr_sem.at[dz], me(0, 0, 1)
         )
 
     def packed(dz):
@@ -258,11 +314,11 @@
                 pltpu.make_async_copy(act.at[i, :, dz], ref.at[:, dz], ao_sem.at[i, dz])
             )
         sent["d", dz] = remote(
-            drs.at[dz], dr.at[dz, :, pl.ds(half, half)], ds_sem.at[dz], dr_sem.at[dz], me(0, 0, 0, 1)
+            drs.at[dz], dr.at[dz, :, pl.ds(half, half)], ds_sem.at[dz], dr_sem.at[dz], me(0, 0, 1)
         )
         sent.pop(("xo", 0, dz)).wait()
         sent.pop(("xo", 1, dz)).wait()
-        pl.semaphore_signal(credit.at[dz], inc=1, device_id=me(0, 0, 0, 1), device_id_type=MESH)
+        pl.semaphore_signal(credit.at[dz], inc=1, device_id=me(0, 0, 1), device_id_type=MESH)
         sent.pop(("p", dz)).wait_send()
 
     def backward(dz, l):
@@ -282,7 +338,7 @@
     def returned(dz):
         pl.semaphore_wait(credit.at[dz], 1)
         sent["s", dz] = remote(
-            xs.at[:, :, dz], x.at[:, :, dz, pl.ds(half, half)], st_sem.at[dz], sr_sem.at[dz], me(0, 0, 0, 1)
+            xs.at[:, :, dz], x.at[:, :, dz, pl.ds(half, half)], st_sem.at[dz], sr_sem.at[dz], me(0, 0, 1)
         )
 
     def put_back(dz):
@@ -293,8 +349,10 @@
         sent.pop(("x", 1, dz, 1)).wait_send()
         if dz == 0:
             for h in range(2):
-                for d in range(1, 4):
-                    sent.pop(("z", h, d)).wait_send()
+                sent.pop(("z", h, 0)).wait_send()
+            passed_on(4)
+        else:
+            passed_on(dz)
         arrive(x.at[:, :, dz, pl.ds(half, half)], sr_sem.at[dz])
         arrive(dr.at[dz, :, pl.ds(half, half)], dr_sem.at[dz])
 
@@ -323,11 +381,14 @@
         for dx in range(2):
             j = dz * 2 + dx
             if j:
-                sent["q", j] = remote(dpart.at[j], dbuf.at[j], qs_sem.at[j], qr_sem.at[j], me(dz, dx))
+                there = place.slot_there(dz) * 2 + dx
+                sent["q", j] = remote(
+                    dpart.at[j], dbuf.at[there], qs_sem.at[j], qr_sem.at[there], place.far(dz, dx)
+                )
 
     def send_wide(dz):
         for h in range(2):
-            across = me(0, 0, 1) if h == 0 else me(0, 1)
+            across = me(0, 1) if h == 0 else me(1)
             for other in (1, 0):
                 dx, dy = (other, 1) if h == 0 else (1, other)
                 sent["w", h, dz, other] = remote(
@@ -349,7 +410,7 @@
                 arrive(wide.at[h, dz, other], wr_sem.at[h, dz, other])
                 add(wide.at[h, dz, other], piece(h, dz, dx, dy))
                 if other:
-                    along = me(0, 1) if h == 0 else me(0, 0, 1)
+                    along = me(1) if h == 0 else me(0, 1)
                     sent["n", h, dz] = remote(
                         wide.at[h, dz, 1], near.at[h, dz], ns_sem.at[h, dz], nr_sem.at[h, dz], along
                     )
@@ -358,77 +419,101 @@
         for h in range(2):
             arrive(near.at[h, dz], nr_sem.at[h, dz])
             add(near.at[h, dz], wide.at[h, dz, 0])
-            if dz:
+            if dz == 3:
+                rows_there = pl.ds(h * half, half)
+                sent["far", h] = start(
+                    pltpu.make_async_copy(near.at[h, 3], far_out.at[:, rows_there], far_sem.at[h])
+                )
+            elif dz:
+                there = place.slot_there(dz)
                 sent["f", h, dz] = remote(
-                    near.at[h, dz], zbuf.at[h, dz - 1], ss_sem.at[h, dz], sz_sem.at[h, dz], me(dz)
+                    near.at[h, dz], zbuf.at[h, there - 1], ss_sem.at[h, dz], sz_sem.at[h, there],
+                    place.far(dz),
                 )
 
-    for h in range(2):
-        by_z(h, 1)
+    own_z()
     column(0)
-    for dz in (2, 3):
-        for h in range(2):
-            by_z(h, dz)
+    loads = {}
+    for l in range(local):
+        for i, (ref, to) in enumerate(((wg_in, wg), (wu_in, wu), (wd_in, wd))):
+            loads[i, l] = start(pltpu.make_async_copy(ref.at[l], to.at[l], w_sem.at[i, l]))
     build_all(0, 8)
     plane(0)
+    pass_on(1)
     column(1)
+    pass_on(2)
     last(0)
+    select(0)
     for dz in range(4):
-        select(dz)
         if dz < 3:
             plane(dz + 1)
+        if dz == 0:
+            pass_on(3)
         packed(dz)
         forward(dz, 0)
         if dz < 2:
             column(dz + 2)
+        if dz == 3:
+            send_near(1)
         forward(dz, 1)
         handed(dz)
-        if dz == 2:
-            send_wide(1)
         backward(dz, 0)
+        if dz == 3:
+            send_near(2)
+            send_z(1)
         backward(dz, 1)
         returned(dz)
-        if dz == 3:
-            send_near(1)
-        put_back(dz)
         if dz < 3:
             last(dz + 1)
-        if dz >= 2:
+            select(dz + 1)
+        put_back(dz)
+        if dz:
             send_wide(dz)
-    send_near(2)
-    send_z(1)
     send_wide(0)
+    send_z(2)
     send_near(3)
-    send_z(2)
+    send_z(3)
 
     total = dpart[0]
     for j in range(1, 8):
         arrive(dbuf.at[j], qr_sem.at[j])
         total = total + dbuf[j]
     dsum[0] = total
-    peer = remote(dsum.at[0], dsum.at[1], qs_sem.at[0], qr_sem.at[0], me(0, 0, 1))
+    peer = remote(dsum.at[0], dsum.at[1], qs_sem.at[0], qr_sem.at[0], me(0, 1))
 
     send_near(0)
-    send_z(3)
     send_z(0)
     arrive(dsum.at[1], qr_sem.at[0])
     dprob_out[...] = dsum[0] + dsum[1]
-    for dz in (1, 2, 3):
-        for h in range(2):
-            arrive(zbuf.at[h, dz - 1], sz_sem.at[h, dz])
-    for a, ref in enumerate((layer_out, dtok_out)):
-        for h in range(2):
-            @pl.loop(0, half // 16)
-            def _(i):
-                at = pl.ds(pl.multiple_of(i * 16, 16), 16)
-                total = near[h, 0, a, at, :].astype(f32)
-                for dz in (1, 2, 3):
-                    total = total + zbuf[h, dz - 1, a, at, :].astype(f32)
-                to = pl.ds(pl.multiple_of(h * half + i * 16, 16), 16)
-                ref[to, :] = total.astype(bf16)
+    for h in range(2):
+        arrive(zbuf.at[h, 0], sz_sem.at[h, 1])
+
+    def finish(others):
+        for a, ref in enumerate((layer_out, dtok_out)):
+            for h in range(2):
+                @pl.loop(0, half // 16)
+                def _(i):
+                    at = pl.ds(pl.multiple_of(i * 16, 16), 16)
+                    total = near[h, 0, a, at, :].astype(f32)
+                    for dz in others:
+                        total = total + zbuf[h, dz - 1, a, at, :].astype(f32)
+                    to = pl.ds(pl.multiple_of(h * half + i * 16, 16), 16)
+                    ref[to, :] = total
+
+    @pl.when(inner)
+    def _():
+        for dz in (2, 3):
+            for h in range(2):
+                arrive(zbuf.at[h, dz - 1], sz_sem.at[h, dz])
+        finish((1, 2, 3))
+
+    @pl.when(jnp.logical_not(inner))
+    def _():
+        finish((1,))
+
     peer.wait_send()
     for key, copy in sent.items():
-        if key[0] == "ao":
+        if key[0] in ("ao", "far"):
             copy.wait()
         else:
             copy.wait_send()
@@ -444,13 +529,14 @@
     shape = jax.ShapeDtypeStruct
     packed = shape((local, 4, rows, full), bf16)
     acts = shape((local, 4, rows, hid), bf16)
-    out = shape((rows, width), bf16)
+    out = shape((rows, width), f32)
+    far = shape((2, rows, width), bf16)
     dma = pltpu.SemaphoreType.DMA
     return pl.pallas_call(
         layer_kernel,
-        out_shape=(packed, packed, acts, acts, acts, out, out, shape((8, rows), f32)),
+        out_shape=(packed, packed, acts, acts, acts, far, out, out, shape((8, rows), f32)),
         in_specs=[any_space, any_space, vmem, any_space, any_space, any_space],
-        out_specs=[any_space] * 5 + [vmem] * 3,
+        out_specs=[any_space] * 6 + [vmem] * 3,
         scratch_shapes=[
             pltpu.VMEM((4, 2, 2, rows, full), bf16),
             pltpu.VMEM((2, 2, 4, rows, full), bf16),
@@ -472,10 +558,10 @@
             pltpu.VMEM((8, 8, rows), f32),
             pltpu.VMEM((8, 8, rows), f32),
             pltpu.VMEM((2, 8, rows), f32),
-            dma((2,)), dma((3, local)), dma((2, 4)), dma((2, 4, 2)), dma((2, 4, 2)), dma((2, 4, 2, 2)),
+            dma((2,)), dma((3, local)), dma((2, 5)), dma((2, 4, 2)), dma((2, 4, 2)), dma((2, 4, 2, 2)),
             dma((8,)), dma((8,)), dma((4,)), dma((4,)), dma((4,)), dma((4,)), dma((4,)), dma((4,)),
             dma((2, 4)), dma((3, 4)), dma((2, 4, 2)), dma((2, 4, 2)), dma((2, 4)), dma((2, 4)),
-            dma((2, 4)), dma((2, 4)), dma((8,)), dma((8,)),
+            dma((2, 4)), dma((2, 4)), dma((8,)), dma((8,)), dma((2,)),
             pltpu.SemaphoreType.REGULAR((4,)),
         ],
         compiler_params=pltpu.CompilerParams(
@@ -484,24 +570,57 @@
     )(tokens, grad_out, routes, w_gate, w_up, w_down)
 
 
+def weight_kernel(hid, dg, du, x, c, wg_out, wu_out, wd_out, turned):
+    @pl.when(pl.program_id(1) == 0)
+    def _():
+        for i, ref in enumerate((hid, dg, du)):
+            turned[i] = ref[0].T
+
+    for i, rows, out in ((1, x, wg_out), (2, x, wu_out), (0, c, wd_out)):
+        out[0] = jnp.dot(turned[i], rows[0], preferred_element_type=jnp.float32)
+
+
+def weights(hidden, d_gate, d_up, x, c):
+    local, rows, hid = hidden.shape
+    full = x.shape[2]
+    tile = 512
+    acts = pl.BlockSpec((1, rows, hid), lambda l, n: (l, 0, 0))
+    ins = pl.BlockSpec((1, rows, tile), lambda l, n: (l, 0, n))
+    out = pl.BlockSpec((1, hid, tile), lambda l, n: (l, 0, n))
+    return pl.pallas_call(
+        weight_kernel,
+        grid=(local, full // tile),
+        out_shape=[jax.ShapeDtypeStruct((local, hid, full), jnp.float32)] * 3,
+        in_specs=[acts] * 3 + [ins] * 2,
+        out_specs=[out] * 3,
+        scratch_shapes=[pltpu.VMEM((3, hid, rows), jnp.bfloat16)],
+        compiler_params=pltpu.CompilerParams(vmem_limit_bytes=60 * 2**20),
+        cost_estimate=pl.CostEstimate(
+            flops=6 * local * hid * rows * full, bytes_accessed=12 * local * hid * full, transcendentals=0
+        ),
+    )(hidden, d_gate, d_up, x, c)
+
+
 def by_one_kernel(tokens, expert_ids, gate_probs, w_gate, w_up, w_down, grad_out):
     topk = expert_ids.shape[1]
     local, hid, full = w_gate.shape
     f32 = jnp.float32
     routes = jnp.concatenate([expert_ids.astype(f32).T, gate_probs.T], axis=0)
-    x, c, hidden, d_gate, d_up, layer_out, d_tokens, d_prob = layer(
+    x, c, hidden, d_gate, d_up, far, layer_out, d_tokens, d_prob = layer(
         tokens, grad_out, routes, w_gate, w_up, w_down
     )
     x, c = (v.reshape(local, -1, full) for v in (x, c))
     hidden, d_gate, d_up = (v.reshape(local, -1, hid) for v in (hidden, d_gate, d_up))
 
-    def weight(rows, values):
-        return jnp.einsum("erh,erd->ehd", rows, values, preferred_element_type=f32)
-
-    return (
-        layer_out, d_tokens, d_prob[:topk].T,
-        weight(d_gate, x), weight(d_up, x), weight(hidden, c),
+    ends = [(z * 4 + i, (3 - z) * 4 + i) for z in (0, 3) for i in range(4)]
+    inners = [(z * 4 + i, (6 - 3 * z) * 4 + i) for z in (1, 2) for i in range(4)]
+    far = [lax.ppermute(far, "fsdp", pairs) for pairs in (ends, inners)]
+    d_w_gate, d_w_up, d_w_down = weights(hidden, d_gate, d_up, x, c)
+    layer_out, d_tokens = (
+        (own + far[0][a].astype(f32) + far[1][a].astype(f32)).astype(tokens.dtype)
+        for a, own in enumerate((layer_out, d_tokens))
     )
+    return (layer_out, d_tokens, d_prob[:topk].T, d_w_gate, d_w_up, d_w_down)
 
 
 def gather_any(value):

time: 212 us -> 190 us (0.90)
  the two profiles are of different devices: /device:TPU:9 before, /device:TPU:0 now
where the time goes in v2:
time: 190 us
  Pallas kernels  178 us (94%)
  waiting for transfers between devices  4.2 us (2%)
  starting transfers between devices  3.21 us (2%)
  other arithmetic  3 us (2%)
    pallas_call x1, Pallas kernels, layer(): pl.pallas_call(layer_kernel, out_shape=(packed, packed, acts, acts, acts,...  158 us
    pallas_call x1, Pallas kernels, weights(): pl.pallas_call(weight_kernel, grid=(local, full // tile), out_shape=[jax....  20.2 us
    ppermute x2, waiting for transfers between devices, by_one_kernel(): far = [lax.ppermute(far, 'fsdp', pairs) for pairs in (ends, inners)]  4.2 us
  transfers between devices with their start and end apart: 2, of which 1 were waited for; matrix products, arithmetic and copies ran while one was open for 0% of the time, Pallas kernels for 11%

profile of v2, /device:TPU:0, one launch (start us, length us, event | category | flops | bytes accessed | tf_op | source)
XLA Modules:
  0.0 189.8 jit_solution(263080375043117229)
XLA Ops:
  0.6 0.7 convert_bitcast_fusion
  1.3 1.3 pad_maximum_fusion.routes_in
  2.6 157.9 %shard_map.118 = (bf16[2,4,128,2048]{3,2,1,0:T(8,128)(2,1)}, bf16[2,4,128,2048]{3,2,1,0:T(8,128)(2,1)}, bf16[2,4,128,704]{3,2,1,0:T(8,128)(2,1)}, bf16[2,4,128,7...) custom-call(bf16[128,1024]{1,0:T(8,128)(2,1)} %tok_in.1, ...), custom_call_target="tpu_custom_call" | custom-call | tf_op jit(solution)/shard_map/pallas_call | solution.py:535
  160.5 1.3 collective-permute-start.1
  161.8 1.9 %collective-permute-start = (bf16[2,128,1024]{2,1,0:T(8,128)(2,1)}, bf16[2,128,1024]{2,1,0:T(8,128)(2,1)S(1)}, u32[]{:S(2)}, u32[]{:S(2)}) collective-permute-start(bf16[2,128,1024]{2,1,0:T(8,128)(2,1)} %get-tuple-element.19), channel_id=1, source_target_pairs={{0,24},{2,26},{4,28},{6,30},{24,0},{26,2},{28,4},{30,6},{1,25},{3,... | collective-permute-start | bytes 1572872 | tf_op jit(solution)/shard_map/ppermute | solution.py:617
  163.8 0.0 copy-start.2
  163.8 0.0 copy-start
  163.8 0.0 copy-start.1
  163.8 20.2 %shard_map.119 = (f32[2,704,2048]{2,1,0:T(8,128)}, f32[2,704,2048]{2,1,0:T(8,128)}, f32[2,704,2048]{2,1,0:T(8,128)}) custom-call(bf16[2,512,704]{2,1,0:T(8,128)(2,1)} %bitcast.33, bf16[2,512,704]{2,1,0:T(8,128)(2,1)} %bitcast.34, bf16[2,512,704]{2,1,0:T(8,128)(2,1)} %bitcast.35, bf16[2,512,2048]{2,1,0:T(8,128)(2,1)} %bitcast.31, bf16[2,512,2048]{2,1,0:T(8,128)(2,1)} %bitcast.32), custom_call_target="tpu_custom_call" | custom-call | flops 8858370048 | bytes 34603008 | tf_op jit(solution)/shard_map/pallas_call | solution.py:590
  183.9 0.0 copy-done.2
  183.9 0.6 slice_bitcast_fusion.4
  184.5 4.2 %collective-permute-done.1 = bf16[2,128,1024]{2,1,0:T(8,128)(2,1)S(1)} collective-permute-done((bf16[2,128,1024]{2,1,0:T(8,128)(2,1)}, bf16[2,128,1024]{2,1,0:T(8,128)(2,1)S(1)}, u32[]{:S(2)}, u32[]{:S(2)}) %collective-permute-start.1) | collective-permute-done | bytes 524320 | tf_op jit(solution)/shard_map/ppermute | solution.py:617
  188.7 0.0 collective-permute-done
  188.7 0.0 copy-done
  188.7 0.0 copy-done.1
  188.7 1.0 fusion
Async XLA Ops:
  160.5 28.2 %collective-permute-start.1 = (bf16[2,128,1024]{2,1,0:T(8,128)(2,1)}, bf16[2,128,1024]{2,1,0:T(8,128)(2,1)S(1)}, u32[]{:S(2)}, u32[]{:S(2)}) collective-permute-start(bf16[2,128,1024]{2,1,0:T(8,128)(2,1)} %get-tuple-element.19), channel_id=1, source_target_pairs={{8,24},{10,26},{12,28},{14,30},{16,0},{18,2},{20,4},{22,6},{9,25},... | collective-permute-start | bytes 1572872 | tf_op jit(solution)/shard_map/ppermute | solution.py:617
  161.8 26.9 %collective-permute-start = (bf16[2,128,1024]{2,1,0:T(8,128)(2,1)}, bf16[2,128,1024]{2,1,0:T(8,128)(2,1)S(1)}, u32[]{:S(2)}, u32[]{:S(2)}) collective-permute-start(bf16[2,128,1024]{2,1,0:T(8,128)(2,1)} %get-tuple-element.19), channel_id=1, source_target_pairs={{0,24},{2,26},{4,28},{6,30},{24,0},{26,2},{28,4},{30,6},{1,25},{3,... | collective-permute-start | bytes 1572872 | tf_op jit(solution)/shard_map/ppermute | solution.py:617
  163.8 20.2 %copy-start.2 = (f32[8,128]{1,0:T(8,128)S(1)}, f32[8,128]{1,0:T(8,128)}, u32[]{:S(2)}) copy-start(f32[8,128]{1,0:T(8,128)} %get-tuple-element.21) | copy-start | bytes 12292
  163.8 25.0 %copy-start = (f32[128,1024]{1,0:T(8,128)S(1)}, f32[128,1024]{1,0:T(8,128)}, u32[]{:S(2)}) copy-start(f32[128,1024]{1,0:T(8,128)} %get-tuple-element.18) | copy-start | bytes 1572868
  163.8 25.0 %copy-start.1 = (f32[128,1024]{1,0:T(8,128)S(1)}, f32[128,1024]{1,0:T(8,128)}, u32[]{:S(2)}) copy-start(f32[128,1024]{1,0:T(8,128)} %get-tuple-element.20) | copy-start | bytes 1572868

commit v3 on v2

--- a/solution.py
+++ b/solution.py
@@ -1,3 +1,5 @@
+import functools
+
 import jax
 import jax.numpy as jnp
 from jax import lax
@@ -76,13 +78,13 @@
 
 def layer_kernel(
     tok_in, grad_in, routes_in, wg_in, wu_in, wd_in,
-    x_out, c_out, hid_out, dg_out, du_out, far_out, layer_out, dtok_out, dprob_out,
+    x_out, c_out, hid_out, dg_out, du_out, far_out, give0, give1, keep0, keep1, layer_out, dtok_out, dprob_out,
     g, x, xs, wg, wu, wd, act, wide, near, zbuf,
     routes, sel, back, row_prob, inverse, dr, drs, dpart, dbuf, dsum,
     own_sem, w_sem, zs_sem, xsend_sem, ysend_sem, recv_sem,
     rs_sem, rr_sem, px_sem, pr_sem, st_sem, sr_sem, ds_sem, dr_sem,
     xo_sem, ao_sem, ws_sem, wr_sem, ns_sem, nr_sem, ss_sem, sz_sem,
-    qs_sem, qr_sem, far_sem, credit,
+    qs_sem, qr_sem, far_sem, own_out_sem, credit,
 ):
     place = Place()
     f32, bf16 = jnp.float32, jnp.bfloat16
@@ -430,6 +432,18 @@
                     near.at[h, dz], zbuf.at[h, there - 1], ss_sem.at[h, dz], sz_sem.at[h, there],
                     place.far(dz),
                 )
+
+    def leave_own():
+        gives, keeps = (give0, give1), (keep0, keep1)
+        for h in range(2):
+            for far, refs in ((1, gives), (0, keeps)):
+                for other in range(2):
+                    dx, dy = (other, far) if h == 0 else (far, other)
+                    sent["own", h, far, other] = start(
+                        pltpu.make_async_copy(
+                            piece(h, 0, dx, dy), refs[h].at[other], own_out_sem.at[h, far, other]
+                        )
+                    )
 
     own_z()
     column(0)
@@ -469,7 +483,8 @@
         put_back(dz)
         if dz:
             send_wide(dz)
-    send_wide(0)
+        else:
+            leave_own()
     send_z(2)
     send_near(3)
     send_z(3)
@@ -481,8 +496,6 @@
     dsum[0] = total
     peer = remote(dsum.at[0], dsum.at[1], qs_sem.at[0], qr_sem.at[0], me(0, 1))
 
-    send_near(0)
-    send_z(0)
     arrive(dsum.at[1], qr_sem.at[0])
     dprob_out[...] = dsum[0] + dsum[1]
     for h in range(2):
@@ -494,7 +507,7 @@
                 @pl.loop(0, half // 16)
                 def _(i):
                     at = pl.ds(pl.multiple_of(i * 16, 16), 16)
-                    total = near[h, 0, a, at, :].astype(f32)
+                    total = zbuf[h, 0, a, at, :].astype(f32)
                     for dz in others:
                         total = total + zbuf[h, dz - 1, a, at, :].astype(f32)
                     to = pl.ds(pl.multiple_of(h * half + i * 16, 16), 16)
@@ -505,15 +518,15 @@
         for dz in (2, 3):
             for h in range(2):
                 arrive(zbuf.at[h, dz - 1], sz_sem.at[h, dz])
-        finish((1, 2, 3))
+        finish((2, 3))
 
     @pl.when(jnp.logical_not(inner))
     def _():
-        finish((1,))
+        finish(())
 
     peer.wait_send()
     for key, copy in sent.items():
-        if key[0] in ("ao", "far"):
+        if key[0] in ("ao", "far", "own"):
             copy.wait()
         else:
             copy.wait_send()
@@ -531,12 +544,13 @@
     acts = shape((local, 4, rows, hid), bf16)
     out = shape((rows, width), f32)
     far = shape((2, rows, width), bf16)
+    quarter = shape((2, 2, half, width), bf16)
     dma = pltpu.SemaphoreType.DMA
     return pl.pallas_call(
         layer_kernel,
-        out_shape=(packed, packed, acts, acts, acts, far, out, out, shape((8, rows), f32)),
+        out_shape=(packed, packed, acts, acts, acts, far) + (quarter,) * 4 + (out, out, shape((8, rows), f32)),
         in_specs=[any_space, any_space, vmem, any_space, any_space, any_space],
-        out_specs=[any_space] * 6 + [vmem] * 3,
+        out_specs=[any_space] * 10 + [vmem] * 3,
         scratch_shapes=[
             pltpu.VMEM((4, 2, 2, rows, full), bf16),
             pltpu.VMEM((2, 2, 4, rows, full), bf16),
@@ -561,7 +575,7 @@
             dma((2,)), dma((3, local)), dma((2, 5)), dma((2, 4, 2)), dma((2, 4, 2)), dma((2, 4, 2, 2)),
             dma((8,)), dma((8,)), dma((4,)), dma((4,)), dma((4,)), dma((4,)), dma((4,)), dma((4,)),
             dma((2, 4)), dma((3, 4)), dma((2, 4, 2)), dma((2, 4, 2)), dma((2, 4)), dma((2, 4)),
-            dma((2, 4)), dma((2, 4)), dma((8,)), dma((8,)), dma((2,)),
+            dma((2, 4)), dma((2, 4)), dma((8,)), dma((8,)), dma((2,)), dma((2, 2, 2)),
             pltpu.SemaphoreType.REGULAR((4,)),
         ],
         compiler_params=pltpu.CompilerParams(
@@ -570,35 +584,39 @@
     )(tokens, grad_out, routes, w_gate, w_up, w_down)
 
 
-def weight_kernel(hid, dg, du, x, c, wg_out, wu_out, wd_out, turned):
+def weight_kernel(count, *refs):
+    acts, rows, outs, turned = refs[:count], refs[count], refs[count + 1 : -1], refs[-1]
+
     @pl.when(pl.program_id(1) == 0)
     def _():
-        for i, ref in enumerate((hid, dg, du)):
+        for i, ref in enumerate(acts):
             turned[i] = ref[0].T
 
-    for i, rows, out in ((1, x, wg_out), (2, x, wu_out), (0, c, wd_out)):
+    for i, out in enumerate(outs):
         out[0] = jnp.dot(turned[i], rows[0], preferred_element_type=jnp.float32)
 
 
-def weights(hidden, d_gate, d_up, x, c):
-    local, rows, hid = hidden.shape
-    full = x.shape[2]
-    tile = 512
-    acts = pl.BlockSpec((1, rows, hid), lambda l, n: (l, 0, 0))
-    ins = pl.BlockSpec((1, rows, tile), lambda l, n: (l, 0, n))
+def weights(acts, values):
+    local, rows, hid = acts[0].shape
+    full = values.shape[2]
+    count, tile = len(acts), 512
+    of_act = pl.BlockSpec((1, rows, hid), lambda l, n: (l, 0, 0))
+    of_rows = pl.BlockSpec((1, rows, tile), lambda l, n: (l, 0, n))
     out = pl.BlockSpec((1, hid, tile), lambda l, n: (l, 0, n))
     return pl.pallas_call(
-        weight_kernel,
+        functools.partial(weight_kernel, count),
         grid=(local, full // tile),
-        out_shape=[jax.ShapeDtypeStruct((local, hid, full), jnp.float32)] * 3,
-        in_specs=[acts] * 3 + [ins] * 2,
-        out_specs=[out] * 3,
-        scratch_shapes=[pltpu.VMEM((3, hid, rows), jnp.bfloat16)],
+        out_shape=[jax.ShapeDtypeStruct((local, hid, full), jnp.float32)] * count,
+        in_specs=[of_act] * count + [of_rows],
+        out_specs=[out] * count,
+        scratch_shapes=[pltpu.VMEM((count, hid, rows), jnp.bfloat16)],
         compiler_params=pltpu.CompilerParams(vmem_limit_bytes=60 * 2**20),
         cost_estimate=pl.CostEstimate(
-            flops=6 * local * hid * rows * full, bytes_accessed=12 * local * hid * full, transcendentals=0
+            flops=2 * count * local * hid * rows * full,
+            bytes_accessed=5 * count * local * hid * full,
+            transcendentals=0,
         ),
-    )(hidden, d_gate, d_up, x, c)
+    )(*acts, values)
 
 
 def by_one_kernel(tokens, expert_ids, gate_probs, w_gate, w_up, w_down, grad_out):
@@ -606,20 +624,34 @@
     local, hid, full = w_gate.shape
     f32 = jnp.float32
     routes = jnp.concatenate([expert_ids.astype(f32).T, gate_probs.T], axis=0)
-    x, c, hidden, d_gate, d_up, far, layer_out, d_tokens, d_prob = layer(
+    x, c, hidden, d_gate, d_up, far, *own, part_out, part_in, d_prob = layer(
         tokens, grad_out, routes, w_gate, w_up, w_down
     )
     x, c = (v.reshape(local, -1, full) for v in (x, c))
     hidden, d_gate, d_up = (v.reshape(local, -1, hid) for v in (hidden, d_gate, d_up))
 
+    blocks = lax.axis_size("fsdp")
+    by_y = functools.partial(lax.ppermute, axis_name="tok", perm=[(0, 1), (1, 0)])
+    by_x = functools.partial(
+        lax.ppermute, axis_name="fsdp", perm=[(i, i + 2 - i // 2 % 2 * 4) for i in range(blocks)]
+    )
+    give0, give1, keep0, keep1 = own
+    near0, near1 = by_y(give0), by_x(give1)
     ends = [(z * 4 + i, (3 - z) * 4 + i) for z in (0, 3) for i in range(4)]
     inners = [(z * 4 + i, (6 - 3 * z) * 4 + i) for z in (1, 2) for i in range(4)]
     far = [lax.ppermute(far, "fsdp", pairs) for pairs in (ends, inners)]
-    d_w_gate, d_w_up, d_w_down = weights(hidden, d_gate, d_up, x, c)
-    layer_out, d_tokens = (
-        (own + far[0][a].astype(f32) + far[1][a].astype(f32)).astype(tokens.dtype)
-        for a, own in enumerate((layer_out, d_tokens))
-    )
+    d_w_gate, d_w_up = weights((d_gate, d_up), x)
+    sum0, sum1 = near0 + keep0, near1 + keep1
+    sum0, sum1, hidden = lax.optimization_barrier((sum0, sum1, hidden))
+    near0, near1 = by_x(sum0[1]), by_y(sum1[1])
+    (d_w_down,) = weights((hidden,), c)
+
+    def total(a, part):
+        halves = [near[a].astype(f32) + held[0, a].astype(f32) for near, held in ((near0, sum0), (near1, sum1))]
+        value = part + jnp.concatenate(halves, axis=0) + far[0][a].astype(f32) + far[1][a].astype(f32)
+        return value.astype(tokens.dtype)
+
+    layer_out, d_tokens = total(0, part_out), total(1, part_in)
     return (layer_out, d_tokens, d_prob[:topk].T, d_w_gate, d_w_up, d_w_down)
 
 

time: 190 us -> 182 us (0.958)
  Pallas kernels: 178 us -> 167 us
  starting transfers between devices: 3.21 us -> 7.67 us
  waiting for transfers between devices: 4.2 us -> 0.02 us
    pallas_call x1, Pallas kernels: 158 us -> 141 us  [layer(): pl.pallas_call(layer_kernel, out_shape=(packed, packed, acts, acts, acts,...]
    pallas_call x1 -> x2, Pallas kernels: 20.2 us -> 25.7 us  [weights(): pl.pallas_call(functools.partial(weight_kernel, count), grid=(local, full...]
    ppermute x0 -> x4, starting transfers between devices: none -> 4.25 us  [the longest x2 2.17 us: by_one_kernel(): near0, near1 = (by_y(give0), by_x(give1))]
    ppermute x2, waiting for transfers between devices: 4.2 us -> 0.01 us  [by_one_kernel(): far = [lax.ppermute(far, 'fsdp', pairs) for pairs in (ends, inners)]]
  transfers between devices with their start and end apart: 2 -> 6, of which waited for: 1 -> 0; matrix products, arithmetic and copies ran while one was open for 0% -> 2% of each run, Pallas kernels for 11% -> 14%
where the time goes in v3:
time: 182 us; the launch traced here: 181 us
  Pallas kernels  167 us (92%)
  starting transfers between devices  7.67 us (4%)
  other arithmetic  4.57 us (3%)
    pallas_call x1, Pallas kernels, layer(): pl.pallas_call(layer_kernel, out_shape=(packed, packed, acts, acts, acts,...  141 us
    pallas_call x2, Pallas kernels, weights(): pl.pallas_call(functools.partial(weight_kernel, count), grid=(local, full...  25.7 us
  transfers between devices with their start and end apart: 6, of which 0 were waited for; matrix products, arithmetic and copies ran while one was open for 2% of the time, Pallas kernels for 14%

profile of v3, /device:TPU:0, one launch (start us, length us, event | category | flops | bytes accessed | tf_op | source)
XLA Modules:
  0.0 181.3 jit_solution(3527022558360111833)
XLA Ops:
  0.6 0.7 convert_bitcast_fusion
  1.3 1.3 pad_maximum_fusion.routes_in
  2.6 141.3 %shard_map.118 = (bf16[2,4,128,2048]{3,2,1,0:T(8,128)(2,1)}, bf16[2,4,128,2048]{3,2,1,0:T(8,128)(2,1)}, bf16[2,4,128,704]{3,2,1,0:T(8,128)(2,1)}, bf16[2,4,128,7...) custom-call(bf16[128,1024]{1,0:T(8,128)(2,1)} %tok_in.1, ...), custom_call_target="tpu_custom_call" | custom-call | tf_op jit(solution)/shard_map/pallas_call | solution.py:549
  143.9 1.3 collective-permute-start.5
  145.2 2.1 %collective-permute-start.4 = (bf16[2,128,1024]{2,1,0:T(8,128)(2,1)}, bf16[2,128,1024]{2,1,0:T(8,128)(2,1)S(1)}, u32[]{:S(2)}, u32[]{:S(2)}) collective-permute-start(bf16[2,128,1024]{2,1,0:T(8,128)(2,1)} %get-tuple-element.32), channel_id=1, source_target_pairs={{0,24},{2,26},{4,28},{6,30},{24,0},{26,2},{28,4},{30,6},{1,25},{3,... | collective-permute-start | bytes 1572872 | tf_op jit(solution)/shard_map/ppermute | solution.py:642
  147.3 1.1 collective-permute-start
  148.4 1.0 collective-permute-start.1
  149.5 1.3 slice_bitcast_fusion.10
  150.7 0.0 copy-start.3
  150.8 0.0 copy-start.2
  150.8 14.7 %shard_map.119 = (f32[2,704,2048]{2,1,0:T(8,128)}, f32[2,704,2048]{2,1,0:T(8,128)}) custom-call(bf16[2,512,704]{2,1,0:T(8,128)(2,1)} %bitcast.70, bf16[2,512,704]{2,1,0:T(8,128)(2,1)} %bitcast.71, bf16[2,512,2048]{2,1,0:T(8,128)(2,1)} %bitcast.69), custom_call_target="tpu_custom_call" | custom-call | flops 5905580032 | bytes 28835840 | tf_op jit(solution)/shard_map/pallas_call | solution.py:606
  165.4 0.0 collective-permute-done
  165.4 0.0 copy-done.3
  165.4 0.2 add.36
  165.6 0.0 collective-permute-done.1
  165.6 0.0 copy-done.2
  165.7 0.2 add.37
  165.9 1.3 collective-permute-start.3
  167.2 0.8 collective-permute-start.2
  168.0 0.0 copy-start
  168.0 0.0 copy-start.1
  168.0 11.0 %shard_map.120 = f32[2,704,2048]{2,1,0:T(8,128)} custom-call(bf16[2,512,704]{2,1,0:T(8,128)(2,1)} %bitcast.67, bf16[2,512,2048]{2,1,0:T(8,128)(2,1)} %bitcast.66), custom_call_target="tpu_custom_call" | custom-call | flops 2952790016 | bytes 14417920 | tf_op jit(solution)/shard_map/pallas_call | solution.py:606
  179.0 0.0 collective-permute-done.3
  179.0 1.0 convert_add_fusion
  180.0 0.0 collective-permute-done.2
  180.0 0.1 convert_add_fusion.1
  180.1 0.0 collective-permute-done.5
  180.1 0.0 collective-permute-done.4
  180.1 0.0 copy-done
  180.1 0.0 copy-done.1
  180.2 1.1 fusion.5
  (2 shorter events, 0.0 us)
Async XLA Ops:
  143.9 36.2 %collective-permute-start.5 = (bf16[2,128,1024]{2,1,0:T(8,128)(2,1)}, bf16[2,128,1024]{2,1,0:T(8,128)(2,1)S(1)}, u32[]{:S(2)}, u32[]{:S(2)}) collective-permute-start(bf16[2,128,1024]{2,1,0:T(8,128)(2,1)} %get-tuple-element.32), channel_id=1, source_target_pairs={{8,24},{10,26},{12,28},{14,30},{16,0},{18,2},{20,4},{22,6},{9,25},... | collective-permute-start | bytes 1572872 | tf_op jit(solution)/shard_map/ppermute | solution.py:642
  145.2 34.9 %collective-permute-start.4 = (bf16[2,128,1024]{2,1,0:T(8,128)(2,1)}, bf16[2,128,1024]{2,1,0:T(8,128)(2,1)S(1)}, u32[]{:S(2)}, u32[]{:S(2)}) collective-permute-start(bf16[2,128,1024]{2,1,0:T(8,128)(2,1)} %get-tuple-element.32), channel_id=1, source_target_pairs={{0,24},{2,26},{4,28},{6,30},{24,0},{26,2},{28,4},{30,6},{1,25},{3,... | collective-permute-start | bytes 1572872 | tf_op jit(solution)/shard_map/ppermute | solution.py:642
  147.3 18.1 %collective-permute-start = (bf16[2,2,64,1024]{3,2,1,0:T(8,128)(2,1)}, bf16[2,2,64,1024]{3,2,1,0:T(8,128)(2,1)S(1)}, u32[]{:S(2)}, u32[]{:S(2)}) collective-permute-start(bf16[2,2,64,1024]{3,2,1,0:T(8,128)(2,1)} %get-tuple-element.25), channel_id=1, source_target_pairs={{0,1},{1,0},{2,3},{3,2},{4,5},{5,4},{6,7},{7,6},{8,9},{9,8},{10,11... | collective-permute-start | bytes 1572872 | tf_op jit(solution)/shard_map/ppermute | solution.py:639
  148.4 17.2 %collective-permute-start.1 = (bf16[2,2,64,1024]{3,2,1,0:T(8,128)(2,1)}, bf16[2,2,64,1024]{3,2,1,0:T(8,128)(2,1)S(1)}, u32[]{:S(2)}, u32[]{:S(2)}) collective-permute-start(bf16[2,2,64,1024]{3,2,1,0:T(8,128)(2,1)} %get-tuple-element.27), channel_id=1, source_target_pairs={{0,4},{2,6},{4,0},{6,2},{8,12},{10,14},{12,8},{14,10},{16,20},{18,... | collective-permute-start | bytes 1572872 | tf_op jit(solution)/shard_map/ppermute | solution.py:639
  150.7 14.7 %copy-start.3 = (bf16[2,2,64,1024]{3,2,1,0:T(8,128)(2,1)S(1)}, bf16[2,2,64,1024]{3,2,1,0:T(8,128)(2,1)}, u32[]{:S(2)}) copy-start(bf16[2,2,64,1024]{3,2,1,0:T(8,128)(2,1)} %get-tuple-element.26) | copy-start | bytes 1572868
  150.8 14.9 %copy-start.2 = (bf16[2,2,64,1024]{3,2,1,0:T(8,128)(2,1)S(1)}, bf16[2,2,64,1024]{3,2,1,0:T(8,128)(2,1)}, u32[]{:S(2)}) copy-start(bf16[2,2,64,1024]{3,2,1,0:T(8,128)(2,1)} %get-tuple-element.28) | copy-start | bytes 1572868
  165.9 13.1 %collective-permute-start.3 = (bf16[2,64,1024]{2,1,0:T(8,128)(2,1)S(1)}, bf16[2,64,1024]{2,1,0:T(8,128)(2,1)}, u32[]{:S(2)}, u32[]{:S(2)}) collective-permute-start(bf16[2,64,1024]{2,1,0:T(8,128)(2,1)S(1)} %slice_bitcast_fusion.4), channel_id=1, source_target_pairs={{0,1},{1,0},{2,3},{3,2},{4,5},{5,4},{6,7},{7,6},{8,9},{9,8},{10,11... | collective-permute-start | bytes 786440 | tf_op jit(solution)/shard_map/ppermute | solution.py:646
  167.2 12.8 %collective-permute-start.2 = (bf16[2,64,1024]{2,1,0:T(8,128)(2,1)S(1)}, bf16[2,64,1024]{2,1,0:T(8,128)(2,1)S(1)}, u32[]{:S(2)}, u32[]{:S(2)}) collective-permute-start(bf16[2,64,1024]{2,1,0:T(8,128)(2,1)S(1)} %slice_bitcast_fusion.5), channel_id=1, source_target_pairs={{0,4},{2,6},{4,0},{6,2},{8,12},{10,14},{12,8},{14,10},{16,20},{18,... | collective-permute-start | bytes 786440 | tf_op jit(solution)/shard_map/ppermute | solution.py:646
  168.0 12.2 %copy-start = (f32[128,1024]{1,0:T(8,128)S(1)}, f32[128,1024]{1,0:T(8,128)}, u32[]{:S(2)}) copy-start(f32[128,1024]{1,0:T(8,128)} %get-tuple-element.24) | copy-start | bytes 1572868
  168.0 12.2 %copy-start.1 = (f32[128,1024]{1,0:T(8,128)S(1)}, f32[128,1024]{1,0:T(8,128)}, u32[]{:S(2)}) copy-start(f32[128,1024]{1,0:T(8,128)} %get-tuple-element.33) | copy-start | bytes 1572868

commit v4 on v3

--- a/solution.py
+++ b/solution.py
@@ -79,7 +79,7 @@
 def layer_kernel(
     tok_in, grad_in, routes_in, wg_in, wu_in, wd_in,
     x_out, c_out, hid_out, dg_out, du_out, far_out, give0, give1, keep0, keep1, layer_out, dtok_out, dprob_out,
-    g, x, xs, wg, wu, wd, act, wide, near, zbuf,
+    g, x, xs, wg, wu, wd, act, turned, wide, near, zbuf,
     routes, sel, back, row_prob, inverse, dr, drs, dpart, dbuf, dsum,
     own_sem, w_sem, zs_sem, xsend_sem, ysend_sem, recv_sem,
     rs_sem, rr_sem, px_sem, pr_sem, st_sem, sr_sem, ds_sem, dr_sem,
@@ -311,10 +311,6 @@
             drs[dz, dx, l * CAP : (l + 1) * CAP, :] = total[half + dx * CAP : half + (dx + 1) * CAP]
 
     def handed(dz):
-        for i, ref in enumerate((hid_out, dg_out, du_out)):
-            sent["ao", i, dz] = start(
-                pltpu.make_async_copy(act.at[i, :, dz], ref.at[:, dz], ao_sem.at[i, dz])
-            )
         sent["d", dz] = remote(
             drs.at[dz], dr.at[dz, :, pl.ds(half, half)], ds_sem.at[dz], dr_sem.at[dz], me(0, 0, 1)
         )
@@ -322,6 +318,19 @@
         sent.pop(("xo", 1, dz)).wait()
         pl.semaphore_signal(credit.at[dz], inc=1, device_id=me(0, 0, 1), device_id_type=MESH)
         sent.pop(("p", dz)).wait_send()
+
+    def turn(dz):
+        refs = (hid_out, dg_out, du_out)
+        for i, ref in enumerate(refs):
+            if dz:
+                sent.pop(("ao", i, dz - 1)).wait()
+            for l in range(local):
+                turned[i, l] = act[i, l, dz].T
+            sent["ao", i, dz] = start(
+                pltpu.make_async_copy(
+                    turned.at[i], ref.at[:, :, pl.ds(dz * rows, rows)], ao_sem.at[i, dz]
+                )
+            )
 
     def backward(dz, l):
         mine = pl.ds(l * CAP, CAP)
@@ -485,6 +494,7 @@
             send_wide(dz)
         else:
             leave_own()
+        turn(dz)
     send_z(2)
     send_near(3)
     send_z(3)
@@ -541,7 +551,7 @@
     vmem = pl.BlockSpec(memory_space=pltpu.VMEM)
     shape = jax.ShapeDtypeStruct
     packed = shape((local, 4, rows, full), bf16)
-    acts = shape((local, 4, rows, hid), bf16)
+    acts = shape((local, hid, 4 * rows), bf16)
     out = shape((rows, width), f32)
     far = shape((2, rows, width), bf16)
     quarter = shape((2, 2, half, width), bf16)
@@ -559,6 +569,7 @@
             pltpu.VMEM((local, hid, full), bf16),
             pltpu.VMEM((local, hid, full), bf16),
             pltpu.VMEM((3, local, 4, rows, hid), bf16),
+            pltpu.VMEM((3, local, hid, rows), bf16),
             pltpu.VMEM((2, 4, 2, 2, half, width), bf16),
             pltpu.VMEM((2, 4, 2, half, width), bf16),
             pltpu.VMEM((2, 3, 2, half, width), bf16),
@@ -585,22 +596,16 @@
 
 
 def weight_kernel(count, *refs):
-    acts, rows, outs, turned = refs[:count], refs[count], refs[count + 1 : -1], refs[-1]
-
-    @pl.when(pl.program_id(1) == 0)
-    def _():
-        for i, ref in enumerate(acts):
-            turned[i] = ref[0].T
-
-    for i, out in enumerate(outs):
-        out[0] = jnp.dot(turned[i], rows[0], preferred_element_type=jnp.float32)
+    acts, rows, outs = refs[:count], refs[count], refs[count + 1 :]
+    for act, out in zip(acts, outs):
+        out[0] = jnp.dot(act[0], rows[0], preferred_element_type=jnp.float32)
 
 
 def weights(acts, values):
-    local, rows, hid = acts[0].shape
+    local, hid, rows = acts[0].shape
     full = values.shape[2]
     count, tile = len(acts), 512
-    of_act = pl.BlockSpec((1, rows, hid), lambda l, n: (l, 0, 0))
+    of_act = pl.BlockSpec((1, hid, rows), lambda l, n: (l, 0, 0))
     of_rows = pl.BlockSpec((1, rows, tile), lambda l, n: (l, 0, n))
     out = pl.BlockSpec((1, hid, tile), lambda l, n: (l, 0, n))
     return pl.pallas_call(
@@ -609,7 +614,6 @@
         out_shape=[jax.ShapeDtypeStruct((local, hid, full), jnp.float32)] * count,
         in_specs=[of_act] * count + [of_rows],
         out_specs=[out] * count,
-        scratch_shapes=[pltpu.VMEM((count, hid, rows), jnp.bfloat16)],
         compiler_params=pltpu.CompilerParams(vmem_limit_bytes=60 * 2**20),
         cost_estimate=pl.CostEstimate(
             flops=2 * count * local * hid * rows * full,
@@ -628,7 +632,6 @@
         tokens, grad_out, routes, w_gate, w_up, w_down
     )
     x, c = (v.reshape(local, -1, full) for v in (x, c))
-    hidden, d_gate, d_up = (v.reshape(local, -1, hid) for v in (hidden, d_gate, d_up))
 
     blocks = lax.axis_size("fsdp")
     by_y = functools.partial(lax.ppermute, axis_name="tok", perm=[(0, 1), (1, 0)])
@@ -644,7 +647,7 @@
     sum0, sum1 = near0 + keep0, near1 + keep1
     sum0, sum1, hidden = lax.optimization_barrier((sum0, sum1, hidden))
     near0, near1 = by_x(sum0[1]), by_y(sum1[1])
-    (d_w_down,) = weights((hidden,), c)
+    d_w_down = jnp.einsum("lhr,lrd->lhd", hidden, c, preferred_element_type=f32)
 
     def total(a, part):
         halves = [near[a].astype(f32) + held[0, a].astype(f32) for near, held in ((near0, sum0), (near1, sum1))]

time: 182 us -> 177 us (0.973)
  Pallas kernels: 167 us -> 155 us
  matrix products: 0 us -> 7.57 us
    pallas_call x2 -> x1, Pallas kernels: 25.7 us -> 13.4 us  [weights(): pl.pallas_call(functools.partial(weight_kernel, count), grid=(local, full...]
    dot_general x0 -> x1, matrix products: none -> 7.57 us  [by_one_kernel(): d_w_down = jnp.einsum('lhr,lrd->lhd', hidden, c, preferred_element_type=f32)]
  transfers between devices with their start and end apart: 6 -> 6, of which waited for: 0 -> 0; matrix products, arithmetic and copies ran while one was open for 2% -> 5% of each run, Pallas kernels for 14% -> 8%
where the time goes in v4:
time: 177 us; the launch traced here: 176 us
  Pallas kernels  155 us (88%)
  starting transfers between devices  7.88 us (4%)
  matrix products  7.57 us (4%)
  other arithmetic  3.62 us (2%)
    pallas_call x1, Pallas kernels, layer(): pl.pallas_call(layer_kernel, out_shape=(packed, packed, acts, acts, acts,...  142 us
    pallas_call x1, Pallas kernels, weights(): pl.pallas_call(functools.partial(weight_kernel, count), grid=(local, full...  13.4 us
    dot_general x1, matrix products, by_one_kernel(): d_w_down = jnp.einsum('lhr,lrd->lhd', hidden, c, preferred_element_type=f32)  7.57 us
    ppermute x2, starting transfers between devices, by_one_kernel(): far = [lax.ppermute(far, 'fsdp', pairs) for pairs in (ends, inners)]  3.64 us
  transfers between devices with their start and end apart: 6, of which 0 were waited for; matrix products, arithmetic and copies ran while one was open for 5% of the time, Pallas kernels for 8%

profile of v4, /device:TPU:0, one launch (start us, length us, event | category | flops | bytes accessed | tf_op | source)
XLA Modules:
  0.0 176.2 jit_solution(15738021581747902507)
XLA Ops:
  0.6 0.7 convert_bitcast_fusion
  1.3 1.3 pad_maximum_fusion.routes_in
  2.6 141.6 %shard_map.118 = (bf16[2,4,128,2048]{3,2,1,0:T(8,128)(2,1)}, bf16[2,4,128,2048]{3,2,1,0:T(8,128)(2,1)}, bf16[2,704,512]{2,1,0:T(8,128)(2,1)}, bf16[2,704,512]{2,...) custom-call(bf16[128,1024]{1,0:T(8,128)(2,1)} %tok_in.1, ...), custom_call_target="tpu_custom_call" | custom-call | tf_op jit(solution)/shard_map/pallas_call | solution.py:559
  144.2 1.3 collective-permute-start.5
  145.5 2.3 %collective-permute-start.4 = (bf16[2,128,1024]{2,1,0:T(8,128)(2,1)}, bf16[2,128,1024]{2,1,0:T(8,128)(2,1)S(1)}, u32[]{:S(2)}, u32[]{:S(2)}) collective-permute-start(bf16[2,128,1024]{2,1,0:T(8,128)(2,1)} %get-tuple-element.32), channel_id=1, source_target_pairs={{0,24},{2,26},{4,28},{6,30},{24,0},{26,2},{28,4},{30,6},{1,25},{3,... | collective-permute-start | bytes 1572872 | tf_op jit(solution)/shard_map/ppermute | solution.py:645
  147.9 1.2 collective-permute-start
  149.1 0.9 collective-permute-start.1
  150.1 1.3 slice_bitcast_fusion.10
  151.3 0.0 copy-start.3
  151.3 0.0 copy-start.2
  151.3 13.4 %shard_map.119 = (f32[2,704,2048]{2,1,0:T(8,128)}, f32[2,704,2048]{2,1,0:T(8,128)}) custom-call(bf16[2,704,512]{2,1,0:T(8,128)(2,1)} %get-tuple-element.35.refs_0_, bf16[2,704,512]{2,1,0:T(8,128)(2,1)} %get-tuple-element.36.refs_1_, bf16[2,512,2048]{2,1,0:T(8,128)(2,1)} %bitcast.67), custom_call_target="tpu_custom_call" | custom-call | flops 5905580032 | bytes 28835840 | tf_op jit(solution)/shard_map/pallas_call | solution.py:611
  164.7 0.0 copy-start.4
  164.7 0.0 collective-permute-done
  164.7 0.0 copy-done.3
  164.7 0.2 add.36
  164.9 0.0 collective-permute-done.1
  164.9 0.0 copy-done.2
  164.9 0.2 add.37
  165.2 1.4 collective-permute-start.3
  166.6 0.7 collective-permute-start.2
  167.3 0.0 copy-done.4
  167.3 0.0 copy-start
  167.3 0.0 copy-start.1
  167.3 7.6 %fusion.6 = f32[2,704,2048]{2,1,0:T(8,128)} fusion(bf16[2,704,512]{2,1,0:T(8,128)(2,1)} %get-tuple-element.40, bf16[2,512,2048]{2,1,0:T(8,128)(2,1)S(1)} %bitcast.66), kind=kOutput, calls=%fused_computation.25 | convolution fusion | flops 2952790016 | bytes 17170432 | tf_op jit(solution)/shard_map/lhr,lrd->lhd/dot_general | solution.py:650
  174.8 0.0 collective-permute-done.3
  174.8 0.1 convert_add_fusion
  174.9 0.0 collective-permute-done.2
  174.9 0.1 convert_add_fusion.1
  175.0 0.0 collective-permute-done.5
  175.0 0.0 collective-permute-done.4
  175.0 0.0 copy-done
  175.0 0.0 copy-done.1
  175.0 1.1 fusion.5
  (2 shorter events, 0.0 us)
Async XLA Ops:
  144.2 30.8 %collective-permute-start.5 = (bf16[2,128,1024]{2,1,0:T(8,128)(2,1)}, bf16[2,128,1024]{2,1,0:T(8,128)(2,1)S(1)}, u32[]{:S(2)}, u32[]{:S(2)}) collective-permute-start(bf16[2,128,1024]{2,1,0:T(8,128)(2,1)} %get-tuple-element.32), channel_id=1, source_target_pairs={{8,24},{10,26},{12,28},{14,30},{16,0},{18,2},{20,4},{22,6},{9,25},... | collective-permute-start | bytes 1572872 | tf_op jit(solution)/shard_map/ppermute | solution.py:645
  145.5 29.5 %collective-permute-start.4 = (bf16[2,128,1024]{2,1,0:T(8,128)(2,1)}, bf16[2,128,1024]{2,1,0:T(8,128)(2,1)S(1)}, u32[]{:S(2)}, u32[]{:S(2)}) collective-permute-start(bf16[2,128,1024]{2,1,0:T(8,128)(2,1)} %get-tuple-element.32), channel_id=1, source_target_pairs={{0,24},{2,26},{4,28},{6,30},{24,0},{26,2},{28,4},{30,6},{1,25},{3,... | collective-permute-start | bytes 1572872 | tf_op jit(solution)/shard_map/ppermute | solution.py:645
  147.9 16.8 %collective-permute-start = (bf16[2,2,64,1024]{3,2,1,0:T(8,128)(2,1)}, bf16[2,2,64,1024]{3,2,1,0:T(8,128)(2,1)S(1)}, u32[]{:S(2)}, u32[]{:S(2)}) collective-permute-start(bf16[2,2,64,1024]{3,2,1,0:T(8,128)(2,1)} %get-tuple-element.25), channel_id=1, source_target_pairs={{0,1},{1,0},{2,3},{3,2},{4,5},{5,4},{6,7},{7,6},{8,9},{9,8},{10,11... | collective-permute-start | bytes 1572872 | tf_op jit(solution)/shard_map/ppermute | solution.py:642
  149.1 15.8 %collective-permute-start.1 = (bf16[2,2,64,1024]{3,2,1,0:T(8,128)(2,1)}, bf16[2,2,64,1024]{3,2,1,0:T(8,128)(2,1)S(1)}, u32[]{:S(2)}, u32[]{:S(2)}) collective-permute-start(bf16[2,2,64,1024]{3,2,1,0:T(8,128)(2,1)} %get-tuple-element.27), channel_id=1, source_target_pairs={{0,4},{2,6},{4,0},{6,2},{8,12},{10,14},{12,8},{14,10},{16,20},{18,... | collective-permute-start | bytes 1572872 | tf_op jit(solution)/shard_map/ppermute | solution.py:642
  151.3 13.4 %copy-start.3 = (bf16[2,2,64,1024]{3,2,1,0:T(8,128)(2,1)S(1)}, bf16[2,2,64,1024]{3,2,1,0:T(8,128)(2,1)}, u32[]{:S(2)}) copy-start(bf16[2,2,64,1024]{3,2,1,0:T(8,128)(2,1)} %get-tuple-element.26) | copy-start | bytes 1572868
  151.3 13.6 %copy-start.2 = (bf16[2,2,64,1024]{3,2,1,0:T(8,128)(2,1)S(1)}, bf16[2,2,64,1024]{3,2,1,0:T(8,128)(2,1)}, u32[]{:S(2)}) copy-start(bf16[2,2,64,1024]{3,2,1,0:T(8,128)(2,1)} %get-tuple-element.28) | copy-start | bytes 1572868
  164.7 2.6 %copy-start.4 = (bf16[2,4,128,2048]{3,2,1,0:T(8,128)(2,1)S(1)}, bf16[2,4,128,2048]{3,2,1,0:T(8,128)(2,1)}, u32[]{:S(2)}) copy-start(bf16[2,4,128,2048]{3,2,1,0:T(8,128)(2,1)} %get-tuple-element.41) | copy-start | bytes 12582916
  165.2 9.7 %collective-permute-start.3 = (bf16[2,64,1024]{2,1,0:T(8,128)(2,1)S(1)}, bf16[2,64,1024]{2,1,0:T(8,128)(2,1)S(1)}, u32[]{:S(2)}, u32[]{:S(2)}) collective-permute-start(bf16[2,64,1024]{2,1,0:T(8,128)(2,1)S(1)} %slice_bitcast_fusion.4), channel_id=1, source_target_pairs={{0,1},{1,0},{2,3},{3,2},{4,5},{5,4},{6,7},{7,6},{8,9},{9,8},{10,11... | collective-permute-start | bytes 786440 | tf_op jit(solution)/shard_map/ppermute | solution.py:649
  166.6 8.3 %collective-permute-start.2 = (bf16[2,64,1024]{2,1,0:T(8,128)(2,1)S(1)}, bf16[2,64,1024]{2,1,0:T(8,128)(2,1)S(1)}, u32[]{:S(2)}, u32[]{:S(2)}) collective-permute-start(bf16[2,64,1024]{2,1,0:T(8,128)(2,1)S(1)} %slice_bitcast_fusion.5), channel_id=1, source_target_pairs={{0,4},{2,6},{4,0},{6,2},{8,12},{10,14},{12,8},{14,10},{16,20},{18,... | collective-permute-start | bytes 786440 | tf_op jit(solution)/shard_map/ppermute | solution.py:649
  167.3 7.7 %copy-start = (f32[128,1024]{1,0:T(8,128)S(1)}, f32[128,1024]{1,0:T(8,128)}, u32[]{:S(2)}) copy-start(f32[128,1024]{1,0:T(8,128)} %get-tuple-element.24) | copy-start | bytes 1572868
  167.3 7.8 %copy-start.1 = (f32[128,1024]{1,0:T(8,128)S(1)}, f32[128,1024]{1,0:T(8,128)}, u32[]{:S(2)}) copy-start(f32[128,1024]{1,0:T(8,128)} %get-tuple-element.33) | copy-start | bytes 1572868

commit v5 on v4

--- a/solution.py
+++ b/solution.py
@@ -470,6 +470,8 @@
     for dz in range(4):
         if dz < 3:
             plane(dz + 1)
+        if dz == 2:
+            send_wide(1)
         if dz == 0:
             pass_on(3)
         packed(dz)
@@ -481,18 +483,18 @@
         forward(dz, 1)
         handed(dz)
         backward(dz, 0)
+        backward(dz, 1)
+        returned(dz)
         if dz == 3:
             send_near(2)
             send_z(1)
-        backward(dz, 1)
-        returned(dz)
         if dz < 3:
             last(dz + 1)
             select(dz + 1)
         put_back(dz)
-        if dz:
+        if dz >= 2:
             send_wide(dz)
-        else:
+        if dz == 0:
             leave_own()
         turn(dz)
     send_z(2)

time: 177 us -> 172 us (0.972)
  Pallas kernels: 155 us -> 149 us
    pallas_call x1, Pallas kernels: 142 us -> 136 us  [layer(): pl.pallas_call(layer_kernel, out_shape=(packed, packed, acts, acts, acts,...]
where the time goes in v5:
time: 172 us; the launch traced here: 171 us
  Pallas kernels  149 us (87%)
  starting transfers between devices  8.64 us (5%)
  matrix products  7.57 us (4%)
  other arithmetic  3.62 us (2%)
    pallas_call x1, Pallas kernels, layer(): pl.pallas_call(layer_kernel, out_shape=(packed, packed, acts, acts, acts,...  136 us
    pallas_call x1, Pallas kernels, weights(): pl.pallas_call(functools.partial(weight_kernel, count), grid=(local, full...  13.4 us
    dot_general x1, matrix products, by_one_kernel(): d_w_down = jnp.einsum('lhr,lrd->lhd', hidden, c, preferred_element_type=f32)  7.57 us
    ppermute x2, starting transfers between devices, by_one_kernel(): far = [lax.ppermute(far, 'fsdp', pairs) for pairs in (ends, inners)]  4.4 us
  transfers between devices with their start and end apart: 6, of which 0 were waited for; matrix products, arithmetic and copies ran while one was open for 5% of the time, Pallas kernels for 8%

profile of v5, /device:TPU:0, one launch (start us, length us, event | category | flops | bytes accessed | tf_op | source)
XLA Modules:
  0.0 171.4 jit_solution(11160465099141652077)
XLA Ops:
  0.6 0.7 convert_bitcast_fusion
  1.3 1.3 pad_maximum_fusion.routes_in
  2.6 136.1 %shard_map.118 = (bf16[2,4,128,2048]{3,2,1,0:T(8,128)(2,1)}, bf16[2,4,128,2048]{3,2,1,0:T(8,128)(2,1)}, bf16[2,704,512]{2,1,0:T(8,128)(2,1)}, bf16[2,704,512]{2,...) custom-call(bf16[128,1024]{1,0:T(8,128)(2,1)} %tok_in.1, ...), custom_call_target="tpu_custom_call" | custom-call | tf_op jit(solution)/shard_map/pallas_call | solution.py:561
  138.7 1.3 collective-permute-start.5
  140.0 3.1 %collective-permute-start.4 = (bf16[2,128,1024]{2,1,0:T(8,128)(2,1)}, bf16[2,128,1024]{2,1,0:T(8,128)(2,1)S(1)}, u32[]{:S(2)}, u32[]{:S(2)}) collective-permute-start(bf16[2,128,1024]{2,1,0:T(8,128)(2,1)} %get-tuple-element.32), channel_id=1, source_target_pairs={{0,24},{2,26},{4,28},{6,30},{24,0},{26,2},{28,4},{30,6},{1,25},{3,... | collective-permute-start | bytes 1572872 | tf_op jit(solution)/shard_map/ppermute | solution.py:647
  143.1 1.1 collective-permute-start
  144.2 0.5 collective-permute-start.1
  144.8 1.3 slice_bitcast_fusion.10
  146.0 0.0 copy-start.3
  146.0 0.0 copy-start.2
  146.0 13.4 %shard_map.119 = (f32[2,704,2048]{2,1,0:T(8,128)}, f32[2,704,2048]{2,1,0:T(8,128)}) custom-call(bf16[2,704,512]{2,1,0:T(8,128)(2,1)} %get-tuple-element.35.refs_0_, bf16[2,704,512]{2,1,0:T(8,128)(2,1)} %get-tuple-element.36.refs_1_, bf16[2,512,2048]{2,1,0:T(8,128)(2,1)} %bitcast.67), custom_call_target="tpu_custom_call" | custom-call | flops 5905580032 | bytes 28835840 | tf_op jit(solution)/shard_map/pallas_call | solution.py:613
  159.4 0.0 copy-start.4
  159.4 0.0 collective-permute-done
  159.4 0.0 copy-done.3
  159.4 0.2 add.36
  159.6 0.0 collective-permute-done.1
  159.6 0.0 copy-done.2
  159.6 0.2 add.37
  159.9 1.6 collective-permute-start.3
  161.4 1.0 collective-permute-start.2
  162.5 0.0 copy-done.4
  162.5 0.0 copy-start
  162.5 0.0 copy-start.1
  162.5 7.6 %fusion.6 = f32[2,704,2048]{2,1,0:T(8,128)} fusion(bf16[2,704,512]{2,1,0:T(8,128)(2,1)} %get-tuple-element.40, bf16[2,512,2048]{2,1,0:T(8,128)(2,1)S(1)} %bitcast.66), kind=kOutput, calls=%fused_computation.25 | convolution fusion | flops 2952790016 | bytes 17170432 | tf_op jit(solution)/shard_map/lhr,lrd->lhd/dot_general | solution.py:652
  170.1 0.0 collective-permute-done.3
  170.1 0.1 convert_add_fusion
  170.1 0.0 collective-permute-done.2
  170.1 0.1 convert_add_fusion.1
  170.2 0.0 collective-permute-done.5
  170.2 0.0 collective-permute-done.4
  170.2 0.0 copy-done
  170.2 0.0 copy-done.1
  170.2 1.1 fusion.5
  (2 shorter events, 0.0 us)
Async XLA Ops:
  138.7 31.5 %collective-permute-start.5 = (bf16[2,128,1024]{2,1,0:T(8,128)(2,1)}, bf16[2,128,1024]{2,1,0:T(8,128)(2,1)S(1)}, u32[]{:S(2)}, u32[]{:S(2)}) collective-permute-start(bf16[2,128,1024]{2,1,0:T(8,128)(2,1)} %get-tuple-element.32), channel_id=1, source_target_pairs={{8,24},{10,26},{12,28},{14,30},{16,0},{18,2},{20,4},{22,6},{9,25},... | collective-permute-start | bytes 1572872 | tf_op jit(solution)/shard_map/ppermute | solution.py:647
  140.0 30.2 %collective-permute-start.4 = (bf16[2,128,1024]{2,1,0:T(8,128)(2,1)}, bf16[2,128,1024]{2,1,0:T(8,128)(2,1)S(1)}, u32[]{:S(2)}, u32[]{:S(2)}) collective-permute-start(bf16[2,128,1024]{2,1,0:T(8,128)(2,1)} %get-tuple-element.32), channel_id=1, source_target_pairs={{0,24},{2,26},{4,28},{6,30},{24,0},{26,2},{28,4},{30,6},{1,25},{3,... | collective-permute-start | bytes 1572872 | tf_op jit(solution)/shard_map/ppermute | solution.py:647
  143.1 16.3 %collective-permute-start = (bf16[2,2,64,1024]{3,2,1,0:T(8,128)(2,1)}, bf16[2,2,64,1024]{3,2,1,0:T(8,128)(2,1)S(1)}, u32[]{:S(2)}, u32[]{:S(2)}) collective-permute-start(bf16[2,2,64,1024]{3,2,1,0:T(8,128)(2,1)} %get-tuple-element.25), channel_id=1, source_target_pairs={{0,1},{1,0},{2,3},{3,2},{4,5},{5,4},{6,7},{7,6},{8,9},{9,8},{10,11... | collective-permute-start | bytes 1572872 | tf_op jit(solution)/shard_map/ppermute | solution.py:644
  144.2 15.4 %collective-permute-start.1 = (bf16[2,2,64,1024]{3,2,1,0:T(8,128)(2,1)}, bf16[2,2,64,1024]{3,2,1,0:T(8,128)(2,1)S(1)}, u32[]{:S(2)}, u32[]{:S(2)}) collective-permute-start(bf16[2,2,64,1024]{3,2,1,0:T(8,128)(2,1)} %get-tuple-element.27), channel_id=1, source_target_pairs={{0,4},{2,6},{4,0},{6,2},{8,12},{10,14},{12,8},{14,10},{16,20},{18,... | collective-permute-start | bytes 1572872 | tf_op jit(solution)/shard_map/ppermute | solution.py:644
  146.0 13.4 %copy-start.3 = (bf16[2,2,64,1024]{3,2,1,0:T(8,128)(2,1)S(1)}, bf16[2,2,64,1024]{3,2,1,0:T(8,128)(2,1)}, u32[]{:S(2)}) copy-start(bf16[2,2,64,1024]{3,2,1,0:T(8,128)(2,1)} %get-tuple-element.26) | copy-start | bytes 1572868
  146.0 13.6 %copy-start.2 = (bf16[2,2,64,1024]{3,2,1,0:T(8,128)(2,1)S(1)}, bf16[2,2,64,1024]{3,2,1,0:T(8,128)(2,1)}, u32[]{:S(2)}) copy-start(bf16[2,2,64,1024]{3,2,1,0:T(8,128)(2,1)} %get-tuple-element.28) | copy-start | bytes 1572868
  159.4 3.1 %copy-start.4 = (bf16[2,4,128,2048]{3,2,1,0:T(8,128)(2,1)S(1)}, bf16[2,4,128,2048]{3,2,1,0:T(8,128)(2,1)}, u32[]{:S(2)}) copy-start(bf16[2,4,128,2048]{3,2,1,0:T(8,128)(2,1)} %get-tuple-element.41) | copy-start | bytes 12582916
  159.9 10.2 %collective-permute-start.3 = (bf16[2,64,1024]{2,1,0:T(8,128)(2,1)S(1)}, bf16[2,64,1024]{2,1,0:T(8,128)(2,1)S(1)}, u32[]{:S(2)}, u32[]{:S(2)}) collective-permute-start(bf16[2,64,1024]{2,1,0:T(8,128)(2,1)S(1)} %slice_bitcast_fusion.4), channel_id=1, source_target_pairs={{0,1},{1,0},{2,3},{3,2},{4,5},{5,4},{6,7},{7,6},{8,9},{9,8},{10,11... | collective-permute-start | bytes 786440 | tf_op jit(solution)/shard_map/ppermute | solution.py:651
  161.4 8.7 %collective-permute-start.2 = (bf16[2,64,1024]{2,1,0:T(8,128)(2,1)S(1)}, bf16[2,64,1024]{2,1,0:T(8,128)(2,1)S(1)}, u32[]{:S(2)}, u32[]{:S(2)}) collective-permute-start(bf16[2,64,1024]{2,1,0:T(8,128)(2,1)S(1)} %slice_bitcast_fusion.5), channel_id=1, source_target_pairs={{0,4},{2,6},{4,0},{6,2},{8,12},{10,14},{12,8},{14,10},{16,20},{18,... | collective-permute-start | bytes 786440 | tf_op jit(solution)/shard_map/ppermute | solution.py:651
  162.5 7.8 %copy-start = (f32[128,1024]{1,0:T(8,128)S(1)}, f32[128,1024]{1,0:T(8,128)}, u32[]{:S(2)}) copy-start(f32[128,1024]{1,0:T(8,128)} %get-tuple-element.24) | copy-start | bytes 1572868
  162.5 7.8 %copy-start.1 = (f32[128,1024]{1,0:T(8,128)S(1)}, f32[128,1024]{1,0:T(8,128)}, u32[]{:S(2)}) copy-start(f32[128,1024]{1,0:T(8,128)} %get-tuple-element.33) | copy-start | bytes 1572868

commit v6 on v5

--- a/solution.py
+++ b/solution.py
@@ -496,7 +496,10 @@
             send_wide(dz)
         if dz == 0:
             leave_own()
-        turn(dz)
+        if dz < 2:
+            turn(dz)
+    turn(2)
+    turn(3)
     send_z(2)
     send_near(3)
     send_z(3)

time: 172 us -> 172 us (level)
  no operation moved by 1% of the time
where the time goes in v6:
time: 172 us; the launch traced here: 171 us
  Pallas kernels  149 us (87%)
  starting transfers between devices  8.64 us (5%)
  matrix products  7.57 us (4%)
  other arithmetic  3.62 us (2%)
    pallas_call x1, Pallas kernels, layer(): pl.pallas_call(layer_kernel, out_shape=(packed, packed, acts, acts, acts,...  136 us
    pallas_call x1, Pallas kernels, weights(): pl.pallas_call(functools.partial(weight_kernel, count), grid=(local, full...  13.4 us
    dot_general x1, matrix products, by_one_kernel(): d_w_down = jnp.einsum('lhr,lrd->lhd', hidden, c, preferred_element_type=f32)  7.57 us
    ppermute x2, starting transfers between devices, by_one_kernel(): far = [lax.ppermute(far, 'fsdp', pairs) for pairs in (ends, inners)]  4.4 us
  transfers between devices with their start and end apart: 6, of which 0 were waited for; matrix products, arithmetic and copies ran while one was open for 5% of the time, Pallas kernels for 8%

profile of v6, /device:TPU:0, one launch (start us, length us, event | category | flops | bytes accessed | tf_op | source)
XLA Modules:
  0.0 171.4 jit_solution(5010106847035207755)
XLA Ops:
  0.6 0.7 convert_bitcast_fusion
  1.3 1.3 pad_maximum_fusion.routes_in
  2.6 136.1 %shard_map.118 = (bf16[2,4,128,2048]{3,2,1,0:T(8,128)(2,1)}, bf16[2,4,128,2048]{3,2,1,0:T(8,128)(2,1)}, bf16[2,704,512]{2,1,0:T(8,128)(2,1)}, bf16[2,704,512]{2,...) custom-call(bf16[128,1024]{1,0:T(8,128)(2,1)} %tok_in.1, ...), custom_call_target="tpu_custom_call" | custom-call | tf_op jit(solution)/shard_map/pallas_call | solution.py:564
  138.7 1.3 collective-permute-start.5
  140.0 3.1 %collective-permute-start.4 = (bf16[2,128,1024]{2,1,0:T(8,128)(2,1)}, bf16[2,128,1024]{2,1,0:T(8,128)(2,1)S(1)}, u32[]{:S(2)}, u32[]{:S(2)}) collective-permute-start(bf16[2,128,1024]{2,1,0:T(8,128)(2,1)} %get-tuple-element.32), channel_id=1, source_target_pairs={{0,24},{2,26},{4,28},{6,30},{24,0},{26,2},{28,4},{30,6},{1,25},{3,... | collective-permute-start | bytes 1572872 | tf_op jit(solution)/shard_map/ppermute | solution.py:650
  143.1 1.1 collective-permute-start
  144.2 0.5 collective-permute-start.1
  144.8 1.3 slice_bitcast_fusion.10
  146.0 0.0 copy-start.3
  146.0 0.0 copy-start.2
  146.0 13.4 %shard_map.119 = (f32[2,704,2048]{2,1,0:T(8,128)}, f32[2,704,2048]{2,1,0:T(8,128)}) custom-call(bf16[2,704,512]{2,1,0:T(8,128)(2,1)} %get-tuple-element.35.refs_0_, bf16[2,704,512]{2,1,0:T(8,128)(2,1)} %get-tuple-element.36.refs_1_, bf16[2,512,2048]{2,1,0:T(8,128)(2,1)} %bitcast.67), custom_call_target="tpu_custom_call" | custom-call | flops 5905580032 | bytes 28835840 | tf_op jit(solution)/shard_map/pallas_call | solution.py:616
  159.4 0.0 copy-start.4
  159.4 0.0 collective-permute-done
  159.4 0.0 copy-done.3
  159.4 0.2 add.36
  159.6 0.0 collective-permute-done.1
  159.6 0.0 copy-done.2
  159.6 0.2 add.37
  159.9 1.6 collective-permute-start.3
  161.4 1.0 collective-permute-start.2
  162.5 0.0 copy-done.4
  162.5 0.0 copy-start
  162.5 0.0 copy-start.1
  162.5 7.6 %fusion.6 = f32[2,704,2048]{2,1,0:T(8,128)} fusion(bf16[2,704,512]{2,1,0:T(8,128)(2,1)} %get-tuple-element.40, bf16[2,512,2048]{2,1,0:T(8,128)(2,1)S(1)} %bitcast.66), kind=kOutput, calls=%fused_computation.25 | convolution fusion | flops 2952790016 | bytes 17170432 | tf_op jit(solution)/shard_map/lhr,lrd->lhd/dot_general | solution.py:655
  170.1 0.0 collective-permute-done.3
  170.1 0.1 convert_add_fusion
  170.1 0.0 collective-permute-done.2
  170.1 0.1 convert_add_fusion.1
  170.2 0.0 collective-permute-done.5
  170.2 0.0 collective-permute-done.4
  170.2 0.0 copy-done
  170.2 0.0 copy-done.1
  170.2 1.1 fusion.5
  (2 shorter events, 0.0 us)
Async XLA Ops:
  138.7 31.5 %collective-permute-start.5 = (bf16[2,128,1024]{2,1,0:T(8,128)(2,1)}, bf16[2,128,1024]{2,1,0:T(8,128)(2,1)S(1)}, u32[]{:S(2)}, u32[]{:S(2)}) collective-permute-start(bf16[2,128,1024]{2,1,0:T(8,128)(2,1)} %get-tuple-element.32), channel_id=1, source_target_pairs={{8,24},{10,26},{12,28},{14,30},{16,0},{18,2},{20,4},{22,6},{9,25},... | collective-permute-start | bytes 1572872 | tf_op jit(solution)/shard_map/ppermute | solution.py:650
  140.0 30.2 %collective-permute-start.4 = (bf16[2,128,1024]{2,1,0:T(8,128)(2,1)}, bf16[2,128,1024]{2,1,0:T(8,128)(2,1)S(1)}, u32[]{:S(2)}, u32[]{:S(2)}) collective-permute-start(bf16[2,128,1024]{2,1,0:T(8,128)(2,1)} %get-tuple-element.32), channel_id=1, source_target_pairs={{0,24},{2,26},{4,28},{6,30},{24,0},{26,2},{28,4},{30,6},{1,25},{3,... | collective-permute-start | bytes 1572872 | tf_op jit(solution)/shard_map/ppermute | solution.py:650
  143.1 16.3 %collective-permute-start = (bf16[2,2,64,1024]{3,2,1,0:T(8,128)(2,1)}, bf16[2,2,64,1024]{3,2,1,0:T(8,128)(2,1)S(1)}, u32[]{:S(2)}, u32[]{:S(2)}) collective-permute-start(bf16[2,2,64,1024]{3,2,1,0:T(8,128)(2,1)} %get-tuple-element.25), channel_id=1, source_target_pairs={{0,1},{1,0},{2,3},{3,2},{4,5},{5,4},{6,7},{7,6},{8,9},{9,8},{10,11... | collective-permute-start | bytes 1572872 | tf_op jit(solution)/shard_map/ppermute | solution.py:647
  144.2 15.4 %collective-permute-start.1 = (bf16[2,2,64,1024]{3,2,1,0:T(8,128)(2,1)}, bf16[2,2,64,1024]{3,2,1,0:T(8,128)(2,1)S(1)}, u32[]{:S(2)}, u32[]{:S(2)}) collective-permute-start(bf16[2,2,64,1024]{3,2,1,0:T(8,128)(2,1)} %get-tuple-element.27), channel_id=1, source_target_pairs={{0,4},{2,6},{4,0},{6,2},{8,12},{10,14},{12,8},{14,10},{16,20},{18,... | collective-permute-start | bytes 1572872 | tf_op jit(solution)/shard_map/ppermute | solution.py:647
  146.0 13.4 %copy-start.3 = (bf16[2,2,64,1024]{3,2,1,0:T(8,128)(2,1)S(1)}, bf16[2,2,64,1024]{3,2,1,0:T(8,128)(2,1)}, u32[]{:S(2)}) copy-start(bf16[2,2,64,1024]{3,2,1,0:T(8,128)(2,1)} %get-tuple-element.26) | copy-start | bytes 1572868
  146.0 13.6 %copy-start.2 = (bf16[2,2,64,1024]{3,2,1,0:T(8,128)(2,1)S(1)}, bf16[2,2,64,1024]{3,2,1,0:T(8,128)(2,1)}, u32[]{:S(2)}) copy-start(bf16[2,2,64,1024]{3,2,1,0:T(8,128)(2,1)} %get-tuple-element.28) | copy-start | bytes 1572868
  159.4 3.1 %copy-start.4 = (bf16[2,4,128,2048]{3,2,1,0:T(8,128)(2,1)S(1)}, bf16[2,4,128,2048]{3,2,1,0:T(8,128)(2,1)}, u32[]{:S(2)}) copy-start(bf16[2,4,128,2048]{3,2,1,0:T(8,128)(2,1)} %get-tuple-element.41) | copy-start | bytes 12582916
  159.9 10.2 %collective-permute-start.3 = (bf16[2,64,1024]{2,1,0:T(8,128)(2,1)S(1)}, bf16[2,64,1024]{2,1,0:T(8,128)(2,1)S(1)}, u32[]{:S(2)}, u32[]{:S(2)}) collective-permute-start(bf16[2,64,1024]{2,1,0:T(8,128)(2,1)S(1)} %slice_bitcast_fusion.4), channel_id=1, source_target_pairs={{0,1},{1,0},{2,3},{3,2},{4,5},{5,4},{6,7},{7,6},{8,9},{9,8},{10,11... | collective-permute-start | bytes 786440 | tf_op jit(solution)/shard_map/ppermute | solution.py:654
  161.4 8.7 %collective-permute-start.2 = (bf16[2,64,1024]{2,1,0:T(8,128)(2,1)S(1)}, bf16[2,64,1024]{2,1,0:T(8,128)(2,1)S(1)}, u32[]{:S(2)}, u32[]{:S(2)}) collective-permute-start(bf16[2,64,1024]{2,1,0:T(8,128)(2,1)S(1)} %slice_bitcast_fusion.5), channel_id=1, source_target_pairs={{0,4},{2,6},{4,0},{6,2},{8,12},{10,14},{12,8},{14,10},{16,20},{18,... | collective-permute-start | bytes 786440 | tf_op jit(solution)/shard_map/ppermute | solution.py:654
  162.5 7.8 %copy-start = (f32[128,1024]{1,0:T(8,128)S(1)}, f32[128,1024]{1,0:T(8,128)}, u32[]{:S(2)}) copy-start(f32[128,1024]{1,0:T(8,128)} %get-tuple-element.24) | copy-start | bytes 1572868
  162.5 7.8 %copy-start.1 = (f32[128,1024]{1,0:T(8,128)S(1)}, f32[128,1024]{1,0:T(8,128)}, u32[]{:S(2)}) copy-start(f32[128,1024]{1,0:T(8,128)} %get-tuple-element.33) | copy-start | bytes 1572868
